TPU v7x, 128 devices: a whole 4x4x4 slice. The times are simulated.
128 devices in a mesh: fsdp: 8 (over z_lo, y), bulk: 16 (over x, z_hi, core).
Axes of the slice: x: 4, y: 4, z: 4 (z_hi: 2, z_lo: 2; z = z_hi * 2 + z_lo), core: 2. Of those that a mesh axis runs over, the one named last changes fastest.
Arguments:
- q_nope: bfloat16 [1536, 8192], P(('fsdp', 'bulk')), may hold values from -0.5 to 0.5
- kv_up: bfloat16 [512, 16384], P(('fsdp', 'bulk')), may hold values from -6 to 6
- o_proj: bfloat16 [8192, 7168], P(('fsdp', 'bulk')), may hold values from -0.5 to 0.5
Outputs:
- q_absorbed: bfloat16 [64, 1536, 512], P('fsdp')
- out_absorbed: bfloat16 [64, 512, 7168], P('fsdp', None, 'bulk')
All inputs are finite; a program needn't handle non-finite values.
Results may differ from a plain program's by a relative error of at most 0.001.
Values may be sent and summed in bfloat16 or wider, within the bound.
No kernel may reach another device: no remote copies, remote signals or barrier semaphores. Data moves between devices by JAX's collectives and lax.ppermute only.
A program may use at most 128 MiB of HBM per device.

v0:
```python
import jax
import jax.numpy as jnp
from jax import lax
from jax.sharding import PartitionSpec as P

QL = 1536
KVL = 512
NOPE = 128
VD = 128


def on_device(q_nope, kv_up, o_proj):
    n_fsdp = lax.axis_size("fsdp")
    q_rows, q_cols = q_nope.shape
    kv_rows, kv_cols = kv_up.shape
    owned_heads = q_cols // n_fsdp // NOPE
    q_send = q_nope.reshape(1, q_rows, n_fsdp, q_cols // n_fsdp)
    kv_send = kv_up.reshape(1, kv_rows, n_fsdp, kv_cols // n_fsdp)
    q_part, kv_part = (
        lax.all_to_all(q_send, "fsdp", split_axis=2, concat_axis=0, tiled=True),
        lax.all_to_all(kv_send, "fsdp", split_axis=2, concat_axis=0, tiled=True),
    )
    q_part = q_part.reshape(n_fsdp, 1, q_rows, q_cols // n_fsdp)
    kv_part = kv_part.reshape(n_fsdp, 1, kv_rows, kv_cols // n_fsdp)
    kv_whole = lax.all_gather(kv_part, "bulk", axis=1, tiled=True)
    latent_full = kv_whole.reshape(KVL, owned_heads, NOPE + VD)
    key_full = latent_full[:, :, :NOPE]
    query_some = q_part.reshape(n_fsdp * q_rows, owned_heads, NOPE)
    query_block = jnp.einsum(
        "rhn,lhn->hrl", query_some, key_full, preferred_element_type=jnp.float32
    )
    query_block = query_block.astype(jnp.bfloat16).reshape(owned_heads, n_fsdp, 1, q_rows, KVL)
    query_whole = lax.all_gather(query_block, "bulk", axis=2, tiled=True)
    q_absorbed = query_whole.reshape(owned_heads, QL, KVL)
    value_full = latent_full[:, :, NOPE:]
    output_rows = lax.all_to_all(o_proj, "bulk", split_axis=1, concat_axis=0, tiled=True)
    output_heads = output_rows.reshape(owned_heads, VD, output_rows.shape[1])
    out_absorbed = jnp.einsum(
        "lhv,hvd->hld", value_full, output_heads, preferred_element_type=jnp.float32
    ).astype(jnp.bfloat16)
    return (q_absorbed, out_absorbed)


def solution(mesh):
    in_specs = (P(("fsdp", "bulk"), None), P(("fsdp", "bulk"), None), P(("fsdp", "bulk"), None))
    out_specs = (P("fsdp", None, None), P("fsdp", None, "bulk"))
    return jax.shard_map(
        on_device, mesh=mesh, in_specs=in_specs, out_specs=out_specs, check_vma=False
    )
```

profile of v0, /device:TPU:1, one launch (start us, length us, event | category | flops | bytes accessed | tf_op | source)
XLA Modules:
  0.0 209.2 jit_solution(4295645533750955701)
XLA Ops:
  7.2 0.0 all-gather.6.cloned.1.call-start
  7.2 11.8 %all_to_all.46 = bf16[1,4,8,2048]{3,1,0,2:T(4,128)(2,1)S(1)} all-to-all(bf16[1,4,8,2048]{3,1,0,2:T(4,128)(2,1)} %bitcast.29), channel_id=1, replica_groups=mesh['fsdp'=8,'bulk'=16] {'fsdp'}, dimensions={2} | all-to-all | bytes 262144 | tf_op jit(solution)/shard_map/all_to_all | solution.py:21
  19.1 0.7 copy.38
  19.8 0.0 all-gather.6.cloned.1.call-update
  19.8 0.0 all-gather.4.cloned.1.call-start
  19.9 1.1 copy.52
  21.0 0.1 copy.37
  21.1 8.7 %all_to_all.47 = bf16[1,12,8,1024]{3,1,0,2:T(8,128)(2,1)S(1)} all-to-all(bf16[1,12,8,1024]{3,1,0,2:T(8,128)(2,1)S(1)} %copy.37), channel_id=1, replica_groups=mesh['fsdp'=8,'bulk'=16] {'fsdp'}, dimensions={2} | all-to-all | bytes 393216 | tf_op jit(solution)/shard_map/all_to_all | solution.py:20
  29.8 0.1 reshape_reshape.3
  29.9 40.3 %all-gather.6.cloned.1.call-done = bf16[8,16,4,1,2048]{4,0,3,2,1:T(8,128)(2,1)} async-done(((bf16[8,1,4,1,2048]{4,0,3,2,1:T(8,128)(2,1)}), bf16[8,16,4,1,2048]{4,0,3,2,1:T(8,128)(2,1)}) %all-gather.6.cloned.1.call-update) | async-done | bytes 2097168 | tf_op jit(solution)/shard_map/all_gather | solution.py:25
  70.2 4.5 %copy.39 = bf16[8,16,4,1,2048]{4,2,1,0,3:T(4,128)(2,1)} copy(bf16[8,16,4,1,2048]{4,0,3,2,1:T(8,128)(2,1)} %all-gather.6.cloned.1.call-done) | data formatting | bytes 4194304 | tf_op jit(solution)/shard_map/all_gather | solution.py:25
  74.7 3.2 %reshape.34 = bf16[512,8,256]{2,1,0:T(8,128)(2,1)S(1)} reshape(bf16[8,16,4,1,2048]{4,2,1,0,3:T(4,128)(2,1)} %copy.39) | data formatting | bytes 4194304 | tf_op jit(solution)/shard_map/reshape | solution.py:26
  78.0 0.1 fusion.3
  78.1 0.0 copy-start
  78.1 0.5 convolution_convert_fusion.1
  78.6 0.4 copy.42
  79.1 1.3 copy.43
  80.4 0.0 all-gather.4.cloned.1.call-update
  80.4 0.0 copy-done
  80.4 1.2 all_to_all.40
  81.7 0.6 copy.46
  82.2 27.5 %all_to_all.48 = bf16[64,16,448]{2,0,1:T(8,128)(2,1)S(1)} all-to-all(bf16[64,16,448]{2,0,1:T(8,128)(2,1)S(1)} %copy.46), channel_id=1, replica_groups=mesh['fsdp'=8,'bulk'=16] {'bulk'}, dimensions={1} | all-to-all | bytes 1835008 | tf_op jit(solution)/shard_map/all_to_all | solution.py:36
  109.7 3.0 %convolution_convert_fusion = bf16[8,512,448]{1,2,0:T(8,128)(2,1)} fusion(bf16[8,128,448]{2,1,0:T(8,128)(2,1)S(1)} %bitcast.23, bf16[512,8,128]{2,1,0:T(8,128)(2,1)S(1)} %get-tuple-element.10), kind=kOutput, calls=%fused_computation | convolution fusion | flops 471597056 | bytes 5636096 | tf_op jit(solution)/shard_map/lhv,hvd->hld/dot_general | solution.py:38
  112.7 65.5 %all-gather.4.cloned.1.call-done = bf16[8,8,16,12,512]{4,1,3,0,2:T(8,128)(2,1)} async-done(((bf16[8,8,1,12,512]{4,1,3,0,2:T(8,128)(2,1)}), bf16[8,8,16,12,512]{4,1,3,0,2:T(8,128)(2,1)}) %all-gather.4.cloned.1.call-update) | async-done | bytes 12582928 | tf_op jit(solution)/shard_map/all_gather | solution.py:33
  178.2 12.0 %copy.44 = bf16[8,8,16,12,512]{4,0,3,2,1:T(8,128)(2,1)S(1)} copy(bf16[8,8,16,12,512]{4,1,3,0,2:T(8,128)(2,1)} %all-gather.4.cloned.1.call-done) | data formatting | bytes 25165824 | tf_op jit(solution)/shard_map/all_gather | solution.py:33
  190.2 12.1 %copy.48 = bf16[8,1536,512]{2,1,0:T(8,128)(2,1)} copy(bf16[8,1536,512]{2,0,1:T(8,128)(2,1)S(1)} %bitcast.22) | data formatting | bytes 25165824
  (1 shorter events, 0.0 us)
Async XLA Ops:
  7.2 63.0 %all-gather.6.cloned.1.call-start = ((), (), s32[]{:S(2)}) async-start(), calls=%async_computation.4 | async-start | bytes 2228224 | tf_op jit(solution)/shard_map/all_gather | solution.py:25
  19.8 158.4 %all-gather.4.cloned.1.call-start = ((), (), s32[]{:S(2)}) async-start(), calls=%async_computation.3 | async-start | bytes 13369344 | tf_op jit(solution)/shard_map/all_gather | solution.py:33
  78.1 2.3 %copy-start = (bf16[64,7168]{1,0:T(8,128)(2,1)S(1)}, bf16[64,7168]{1,0:T(8,128)(2,1)}, u32[]{:S(2)}) copy-start(bf16[64,7168]{1,0:T(8,128)(2,1)} %param.5) | copy-start | bytes 2752516
Sparse Core Ops, SparseCore 0:
  19.9 50.2 all-gather.5
  80.5 97.6 all-gather.3
where the time goes:
time: 210 us; the launch traced here: 209 us
  waiting for transfers between devices  106 us (50%)
  blocking collectives  48 us (23%)
  local copies, waits for them, and re-layouts  37.7 us (18%)
  between operations  14.1 us (7%)
  matrix products  3.49 us (2%)
    all_gather x1, waiting for transfers between devices, on_device(): query_whole = lax.all_gather(query_block, 'bulk', axis=2, tiled=True)  65.5 us
    all_gather x1, waiting for transfers between devices, on_device(): kv_whole = lax.all_gather(kv_part, 'bulk', axis=1, tiled=True)  40.3 us
    all_to_all x1, blocking collectives, on_device(): lax.all_to_all(o_proj, 'bulk', split_axis=1, concat_axis=0, tiled=True)  27.5 us
    unnamed x4, local copies, waits for them, and re-layouts  13.3 us
    all_gather x1, local copies, waits for them, and re-layouts, on_device(): query_whole = lax.all_gather(query_block, 'bulk', axis=2, tiled=True)  12 us
    all_to_all x1, blocking collectives, on_device(): lax.all_to_all(kv_send, 'fsdp', split_axis=2, concat_axis=0, tiled=True)  11.8 us
    all_to_all x1, blocking collectives, on_device(): lax.all_to_all(q_send, 'fsdp', split_axis=2, concat_axis=0, tiled=True)  8.66 us
    all_gather x1, local copies, waits for them, and re-layouts, on_device(): kv_whole = lax.all_gather(kv_part, 'bulk', axis=1, tiled=True)  4.53 us
  transfers between devices with their start and end apart: 2, of which 2 were waited for; matrix products, arithmetic and copies ran while one was open for 2% of the time, Pallas kernels for 0%

commit v1 on v0

v1 whole, which is shorter than its diff:
```python
import jax
import jax.numpy as jnp
from jax import lax
from jax.sharding import PartitionSpec as P

QL = 1536
KVL = 512
NOPE = 128
VD = 128


def on_device(q_nope, kv_up, o_proj):
    n_fsdp = lax.axis_size("fsdp")
    q_rows, q_cols = q_nope.shape
    kv_rows, kv_cols = kv_up.shape
    n_bulk = lax.axis_size("bulk")
    own_cols = q_cols // n_fsdp
    heads = own_cols // NOPE
    q_send = q_nope.reshape(q_rows, n_fsdp, own_cols).transpose(1, 0, 2)
    kv_send = kv_up.reshape(kv_rows, n_fsdp, kv_cols // n_fsdp).transpose(1, 0, 2)
    kv_part = lax.all_to_all(kv_send, "fsdp", split_axis=0, concat_axis=0, tiled=True)
    q_part = lax.all_to_all(q_send, "fsdp", split_axis=0, concat_axis=0, tiled=True)
    kv_all = lax.all_gather(kv_part.reshape(n_fsdp * kv_rows, -1), "bulk", axis=0)
    q_all = lax.all_gather(q_part.reshape(n_fsdp * q_rows, -1), "bulk", axis=0)
    output_rows = lax.all_to_all(o_proj, "bulk", split_axis=1, concat_axis=0, tiled=True)
    latent = kv_all.reshape(n_bulk, n_fsdp, kv_rows, -1).transpose(1, 0, 2, 3)
    latent = latent.reshape(KVL, heads, NOPE + VD)
    query = q_all.reshape(n_bulk, n_fsdp, q_rows, -1).transpose(1, 0, 2, 3)
    query = query.reshape(QL, heads, NOPE)
    q_absorbed = jnp.einsum(
        "rhn,lhn->hrl", query, latent[:, :, :NOPE], preferred_element_type=jnp.float32
    ).astype(jnp.bfloat16)
    output_heads = output_rows.reshape(heads, VD, output_rows.shape[1])
    out_absorbed = jnp.einsum(
        "lhv,hvd->hld", latent[:, :, NOPE:], output_heads, preferred_element_type=jnp.float32
    ).astype(jnp.bfloat16)
    return (q_absorbed, out_absorbed)


def solution(mesh):
    in_specs = (P(("fsdp", "bulk"), None), P(("fsdp", "bulk"), None), P(("fsdp", "bulk"), None))
    out_specs = (P("fsdp", None, None), P("fsdp", None, "bulk"))
    return jax.shard_map(
        on_device, mesh=mesh, in_specs=in_specs, out_specs=out_specs, check_vma=False
    )
```

time: 210 us -> 155 us (0.74)
  waiting for transfers between devices: 106 us -> 68.1 us
  blocking collectives: 48 us -> 20.6 us
  starting transfers between devices: 0.08 us -> 10.6 us
  local copies, waits for them, and re-layouts: 37.7 us -> 28.8 us
  matrix products: 3.49 us -> 12.1 us
    all_gather x2, waiting for transfers between devices: 106 us -> 68.1 us  [the longest x1 37.1 us: on_device(): q_all = lax.all_gather(q_part.reshape(n_fsdp * q_rows, -1), 'bulk', axis=0)]
    all_to_all x3 -> x2, blocking collectives: 48 us -> 20.6 us  [the longest x1 12 us: on_device(): lax.all_to_all(kv_send, 'fsdp', split_axis=0, concat_axis=0, tiled=True)]
    all_gather x2 -> x1, local copies, waits for them, and re-layouts: 16.5 us -> 3.61 us  [on_device(): q_all = lax.all_gather(q_part.reshape(n_fsdp * q_rows, -1), 'bulk', axis=0)]
    unnamed x4 -> x3, local copies, waits for them, and re-layouts: 13.3 us -> 1.11 us
    all_to_all x0 -> x1, starting transfers between devices: none -> 10.6 us  [on_device(): lax.all_to_all(o_proj, 'bulk', split_axis=1, concat_axis=0, tiled=True)]
    reshape x4 -> x6, local copies, waits for them, and re-layouts: 4.68 us -> 14.3 us  [the longest x1 5.56 us: on_device(): query = query.reshape(QL, heads, NOPE)]
    dot_general x2, matrix products: 3.49 us -> 12.1 us  [the longest x1 7.87 us: on_device(): jnp.einsum('rhn,lhn->hrl', query, latent[:, :, :NOPE], preferred_element_...]
    transpose x0 -> x1, local copies, waits for them, and re-layouts: none -> 4.02 us  [on_device(): query = q_all.reshape(n_bulk, n_fsdp, q_rows, -1).transpose(1, 0, 2, 3)]
  transfers between devices with their start and end apart: 2 -> 3, of which waited for: 2 -> 2; matrix products, arithmetic and copies ran while one was open for 2% -> 12% of each run, Pallas kernels for 0% -> 0%
where the time goes in v1:
time: 155 us; the launch traced here: 154 us
  waiting for transfers between devices  68.1 us (44%)
  local copies, waits for them, and re-layouts  28.8 us (19%)
  blocking collectives  20.6 us (13%)
  between operations  14.1 us (9%)
  matrix products  12.1 us (8%)
  starting transfers between devices  10.6 us (7%)
    all_gather x1, waiting for transfers between devices, on_device(): q_all = lax.all_gather(q_part.reshape(n_fsdp * q_rows, -1), 'bulk', axis=0)  37.1 us
    all_gather x1, waiting for transfers between devices, on_device(): lax.all_gather(kv_part.reshape(n_fsdp * kv_rows, -1), 'bulk', axis=0)  31 us
    all_to_all x1, blocking collectives, on_device(): lax.all_to_all(kv_send, 'fsdp', split_axis=0, concat_axis=0, tiled=True)  12 us
    all_to_all x1, starting transfers between devices, on_device(): lax.all_to_all(o_proj, 'bulk', split_axis=1, concat_axis=0, tiled=True)  10.6 us
    all_to_all x1, blocking collectives, on_device(): lax.all_to_all(q_send, 'fsdp', split_axis=0, concat_axis=0, tiled=True)  8.66 us
    dot_general x1, matrix products, on_device(): jnp.einsum('rhn,lhn->hrl', query, latent[:, :, :NOPE], preferred_element_...  7.87 us
    reshape x1, local copies, waits for them, and re-layouts, on_device(): query = query.reshape(QL, heads, NOPE)  5.56 us
    reshape x2, local copies, waits for them, and re-layouts, on_device(): latent = kv_all.reshape(n_bulk, n_fsdp, kv_rows, -1).transpose(1, 0, 2, 3)  5.41 us
  transfers between devices with their start and end apart: 3, of which 2 were waited for; matrix products, arithmetic and copies ran while one was open for 12% of the time, Pallas kernels for 0%

profile of v1, /device:TPU:1, one launch (start us, length us, event | category | flops | bytes accessed | tf_op | source)
XLA Modules:
  0.0 154.4 jit_solution(18130601976197341788)
XLA Ops:
  7.2 0.0 copy-start
  7.2 0.0 all-gather.5.cloned.1.call-start
  7.2 12.0 %all_to_all.26 = bf16[8,4,2048]{2,1,0:T(4,128)(2,1)S(1)} all-to-all(bf16[8,4,2048]{2,1,0:T(4,128)(2,1)} %bitcast.25), channel_id=1, replica_groups=mesh['fsdp'=8,'bulk'=16] {'fsdp'}, dimensions={0} | all-to-all | bytes 262144 | tf_op jit(solution)/shard_map/all_to_all | solution.py:21
  19.2 0.7 all_gather_reshape.7
  19.9 0.0 all-gather.5.cloned.1.call-update
  19.9 0.0 all-gather.3.cloned.1.call-start
  20.0 1.1 copy.28
  21.1 0.1 copy.38
  21.2 8.7 %all_to_all.27 = bf16[8,12,1024]{2,1,0:T(8,128)(2,1)S(1)} all-to-all(bf16[8,12,1024]{2,1,0:T(8,128)(2,1)S(1)} %bitcast.22), channel_id=1, replica_groups=mesh['fsdp'=8,'bulk'=16] {'fsdp'}, dimensions={0} | all-to-all | bytes 393216 | tf_op jit(solution)/shard_map/all_to_all | solution.py:22
  29.9 0.7 all_gather_reshape.6
  30.6 0.0 all-gather.3.cloned.1.call-update
  30.6 0.0 copy-done
  30.6 1.2 all_to_all.20
  31.9 1.6 %copy.23 = bf16[64,16,448]{2,0,1:T(8,128)(2,1)} copy(bf16[64,16,448]{2,1,0:T(8,128)(2,1)S(1)} %all_to_all.20) | data formatting | bytes 1835008 | tf_op jit(solution)/shard_map/all_to_all | solution.py:25
  33.4 10.6 %all-to-all-start.2 = ((bf16[64,16,448]{2,0,1:T(8,128)(2,1)}), bf16[64,16,448]{2,0,1:T(8,128)(2,1)S(1)}, u32[]{:S(2)}, u32[]{:S(2)}) async-start(bf16[64,16,448]{2,0,1:T(8,128)(2,1)} %copy.23), calls=%async_computation.2 | async-start | bytes 2097152 | tf_op jit(solution)/shard_map/all_to_all | solution.py:25
  44.0 31.0 %all-gather.5.cloned.1.call-done = bf16[16,32,2048]{2,1,0:T(8,128)(2,1)} async-done(((bf16[1,32,2048]{2,1,0:T(8,128)(2,1)}), bf16[16,32,2048]{2,1,0:T(8,128)(2,1)}) %all-gather.5.cloned.1.call-update) | async-done | bytes 2097168 | tf_op jit(solution)/shard_map/all_gather | solution.py:23
  75.0 2.7 %reshape.33 = bf16[16,8,4,2048]{3,2,1,0:T(4,128)(2,1)S(1)} reshape(bf16[16,32,2048]{2,1,0:T(8,128)(2,1)} %all-gather.5.cloned.1.call-done) | data formatting | bytes 4194304 | tf_op jit(solution)/shard_map/reshape | solution.py:26
  77.7 2.7 %copy.37 = bf16[16,8,4,2048]{3,2,0,1:T(4,128)(2,1)} copy(bf16[16,8,4,2048]{3,2,1,0:T(4,128)(2,1)S(1)} %reshape.33) | data formatting | bytes 4194304 | tf_op jit(solution)/shard_map/reshape | solution.py:26
  80.4 3.2 %reshape.34 = bf16[512,8,256]{2,1,0:T(8,128)(2,1)S(1)} reshape(bf16[8,16,4,2048]{3,2,1,0:T(4,128)(2,1)} %bitcast.20) | data formatting | bytes 4194304 | tf_op jit(solution)/shard_map/reshape | solution.py:27
  83.6 1.5 fusion.3
  85.1 0.0 all-to-all-done.2
  85.1 4.2 %convolution_convert_fusion.1 = bf16[8,512,448]{1,2,0:T(8,128)(2,1)} fusion(bf16[8,128,448]{2,1,0:T(8,128)(2,1)S(1)} %bitcast.21, bf16[512,8,128]{2,1,0:T(8,128)(2,1)} %get-tuple-element.2), kind=kOutput, calls=%fused_computation.2 | convolution fusion | flops 471597056 | bytes 5636096 | tf_op jit(solution)/shard_map/lhv,hvd->hld/dot_general | solution.py:34
  89.3 37.1 %all-gather.3.cloned.1.call-done = bf16[16,96,1024]{2,1,0:T(8,128)(2,1)} async-done(((bf16[1,96,1024]{2,1,0:T(8,128)(2,1)}), bf16[16,96,1024]{2,1,0:T(8,128)(2,1)}) %all-gather.3.cloned.1.call-update) | async-done | bytes 3145744 | tf_op jit(solution)/shard_map/all_gather | solution.py:24
  126.5 3.6 %copy.16 = bf16[16,96,1024]{2,0,1:T(8,128)(2,1)S(1)} copy(bf16[16,96,1024]{2,1,0:T(8,128)(2,1)} %all-gather.3.cloned.1.call-done) | data formatting | bytes 6291456 | tf_op jit(solution)/shard_map/all_gather | solution.py:24
  130.1 4.0 %copy.17 = bf16[8,16,12,1024]{3,2,1,0:T(8,128)(2,1)} copy(bf16[8,16,12,1024]{3,1,2,0:T(8,128)(2,1)S(1)} %bitcast.19) | data formatting | bytes 6291456 | tf_op jit(solution)/shard_map/transpose | solution.py:28
  134.1 5.6 %reshape.31 = bf16[1536,8,128]{2,1,0:T(8,128)(2,1)S(1)} reshape(bf16[8,16,12,1024]{3,2,1,0:T(8,128)(2,1)} %copy.17) | data formatting | bytes 6291456 | tf_op jit(solution)/shard_map/reshape | solution.py:29
  139.7 7.9 %convolution_convert_fusion = bf16[8,1536,512]{2,1,0:T(8,128)(2,1)} fusion(bf16[1536,8,128]{2,1,0:T(8,128)(2,1)S(1)} %reshape.31, bf16[512,8,128]{2,1,0:T(8,128)(2,1)} %get-tuple-element.3), kind=kOutput, calls=%fused_computation | convolution fusion | flops 1616904192 | bytes 16777216 | tf_op jit(solution)/shard_map/rhn,lhn->hrl/dot_general | solution.py:30
  (1 shorter events, 0.0 us)
Async XLA Ops:
  7.2 23.4 %copy-start = (bf16[64,7168]{1,0:T(8,128)(2,1)S(1)}, bf16[64,7168]{1,0:T(8,128)(2,1)}, u32[]{:S(2)}) copy-start(bf16[64,7168]{1,0:T(8,128)(2,1)} %param.5) | copy-start | bytes 2752516
  7.2 67.8 %all-gather.5.cloned.1.call-start = ((), (), s32[]{:S(2)}) async-start(), calls=%async_computation.4 | async-start | bytes 2228224 | tf_op jit(solution)/shard_map/all_gather | solution.py:23
  19.9 106.6 %all-gather.3.cloned.1.call-start = ((), (), s32[]{:S(2)}) async-start(), calls=%async_computation.3 | async-start | bytes 3342336 | tf_op jit(solution)/shard_map/all_gather | solution.py:24
  33.4 51.7 %all-to-all-start.2 = ((bf16[64,16,448]{2,0,1:T(8,128)(2,1)}), bf16[64,16,448]{2,0,1:T(8,128)(2,1)S(1)}, u32[]{:S(2)}, u32[]{:S(2)}) async-start(bf16[64,16,448]{2,0,1:T(8,128)(2,1)} %copy.23), calls=%async_computation.2 | async-start | bytes 2097152 | tf_op jit(solution)/shard_map/all_to_all | solution.py:25
Sparse Core Ops, SparseCore 0:
  20.0 54.8 all-gather.4
  77.3 49.0 all-gather.2

commit v2 on v1

v2 whole, which is shorter than its diff:
```python
import functools

import jax
import jax.numpy as jnp
import numpy as np
from jax import lax
from jax.experimental import pallas as pl
from jax.experimental.pallas import tpu as pltpu
from jax.sharding import Mesh, PartitionSpec as P

QL = 1536
KVL = 512
NOPE = 128
VD = 128
X, ZH, ZL, Y, C = 4, 2, 2, 4, 2
BULK = ("x", "zh", "c")
F = ZL * Y
HALF = 4
Q_BLOCK = ZH * C * 12
L_BLOCK = ZH * C * 4
MSG_ROWS = Q_BLOCK + 2 * L_BLOCK
D_PART = 448


def shifts(dx, dz, dc):
    at = lambda x, z, c: (x * ZH + z) * C + c
    return [
        (at(x, z, c), at((x + dx) % X, (z + dz) % ZH, (c + dc) % C))
        for x in range(X)
        for z in range(ZH)
        for c in range(C)
    ]


def absorb_kernel(s_ref, *refs):
    m_refs, o_refs, rest = refs[:4], refs[4:8], refs[8:]
    q_out, d_out, kv = rest[-3:]
    i = pl.program_id(0)
    x, zh, c, base = s_ref[0], s_ref[1], s_ref[2], s_ref[3]
    q_cols = pl.ds(pl.multiple_of(i * NOPE, NOPE), NOPE)
    kv_cols = pl.ds(pl.multiple_of((i % 2) * 256, 256), 256)
    kv_rows = pl.ds(pl.multiple_of(Q_BLOCK + (i // 2) * L_BLOCK, L_BLOCK), L_BLOCK)
    for d in range(X):
        xs = lax.rem(x - d + X, X)
        for f in range(F):
            at = pl.multiple_of(f * (X * L_BLOCK) + xs * L_BLOCK, L_BLOCK)
            kv[pl.ds(at, L_BLOCK), :] = m_refs[d][f, kv_rows, kv_cols]
    key = kv[:, :NOPE]
    for d in range(X):
        xs = lax.rem(x - d + X, X)
        query = m_refs[d][:, :Q_BLOCK, q_cols].reshape(F * Q_BLOCK, NOPE)
        block = lax.dot_general(
            query, key, (((1,), (1,)), ((), ())), preferred_element_type=jnp.float32
        ).astype(jnp.bfloat16)
        for f in range(F):
            at = pl.multiple_of(f * (X * Q_BLOCK) + xs * Q_BLOCK, 16)
            q_out[0, pl.ds(at, Q_BLOCK), :] = block[f * Q_BLOCK : (f + 1) * Q_BLOCK]
    value = kv[:, NOPE:]
    head = base + i
    same_z = (head % ZH) == zh
    for core in range(C):

        @pl.when(c == core)
        def _():
            cols = slice(core * 384, core * 384 + 512)
            own = jnp.where(same_z, o_refs[0][0, :, cols], o_refs[1][0, :, cols])
            other = jnp.where(same_z, o_refs[2][0, :, cols], o_refs[3][0, :, cols])
            rows = (own, other) if core == 0 else (other, own)
            out_head = jnp.concatenate(rows, axis=0)
            block = lax.dot_general(
                out_head, value, (((0,), (1,)), ((), ())), preferred_element_type=jnp.float32
            ).astype(jnp.bfloat16)
            d_out[0] = block[core * 64 : core * 64 + D_PART]


def absorb(scalars, messages, o_parts, earlier=None):
    def o_index(i, s):
        return (lax.rem(s[0] - (s[3] + i) // ZH + X, X), 0, 0)

    whole = pl.BlockSpec((F, MSG_ROWS, HALF * NOPE), lambda i, s: (0, 0, 0))
    o_spec = pl.BlockSpec((1, 64, 2 * D_PART), o_index)
    in_specs = [whole] * 4 + [o_spec] * 4
    operands = [*messages, *o_parts]
    aliases = {}
    if earlier is not None:
        in_specs += [pl.BlockSpec(memory_space=pl.ANY)] * 2
        operands += list(earlier)
        aliases = {9: 0, 10: 1}
    return pl.pallas_call(
        absorb_kernel,
        grid_spec=pltpu.PrefetchScalarGridSpec(
            num_scalar_prefetch=1,
            grid=(HALF,),
            in_specs=in_specs,
            out_specs=[
                pl.BlockSpec((1, QL, KVL), lambda i, s: (s[3] + i, 0, 0)),
                pl.BlockSpec((1, D_PART, KVL), lambda i, s: (s[3] + i, 0, 0)),
            ],
            scratch_shapes=[pltpu.VMEM((KVL, NOPE + VD), jnp.bfloat16)],
        ),
        out_shape=[
            jax.ShapeDtypeStruct((2 * HALF, QL, KVL), jnp.bfloat16),
            jax.ShapeDtypeStruct((2 * HALF, D_PART, KVL), jnp.bfloat16),
        ],
        input_output_aliases=aliases,
        compiler_params=pltpu.CompilerParams(vmem_limit_bytes=24 * 2**20),
        cost_estimate=pl.CostEstimate(
            flops=2 * HALF * NOPE * KVL * (QL + 512),
            bytes_accessed=HALF * 2 * KVL * (QL + D_PART) + 4 * 655360,
            transcendentals=0,
        ),
    )(scalars, *operands)


def on_device(q_nope, kv_up, o_proj):
    x, zh, c = lax.axis_index("x"), lax.axis_index("zh"), lax.axis_index("c")
    over = lambda a, *d: lax.ppermute(a, BULK, shifts(*d))

    o_cols = o_proj.shape[1] // X
    o_of = lambda d: lax.dynamic_slice_in_dim(o_proj, lax.rem(x + d, X) * o_cols, o_cols, 1)
    o_x = {d: over(o_of(d), d, 0, 0) for d in (2, 1, 3)}
    o_x[0] = o_of(0)

    q = q_nope.reshape(3, 4, F * C, HALF * NOPE).transpose(2, 0, 1, 3)
    kv = kv_up.reshape(4, F * C, 2, HALF * NOPE).transpose(1, 2, 0, 3)
    send = jnp.concatenate([q, kv], axis=1).reshape(F, 1, C, 5, 4, HALF * NOPE)
    send = jnp.broadcast_to(send, (F, ZH, C, 5, 4, HALF * NOPE)).reshape(F * ZH * C, 5, 4, -1)
    part = lax.all_to_all(send, ("zl", "y", "zh", "c"), split_axis=0, concat_axis=0, tiled=True)
    part = part.reshape(F, ZH * C, 5, 4, HALF * NOPE)
    part_q = part[:, :, :3].reshape(F, Q_BLOCK, HALF * NOPE)
    part_kv = part[:, :, 3:].transpose(0, 2, 1, 3, 4).reshape(F, 2 * L_BLOCK, HALF * NOPE)
    message = jnp.concatenate([part_q, part_kv], axis=1)

    own = [message] + [None] * 3
    for d in (2, 1, 3):
        own[d] = over(message, d, 0, 0)
    o_x = jnp.stack([o_x[d] for d in range(X)])
    half = lambda z: lax.dynamic_slice_in_dim(o_x, z * (2 * D_PART), 2 * D_PART, 2)
    o_own = half(zh)
    o_other = over(half(1 - zh), 0, 1, 0)
    o_parts = [o_own, o_other, over(o_own, 0, 0, 1), over(o_other, 0, 0, 1)]
    other = [over(m, 0, 0, 1) for m in own]

    scalars = lambda base: jnp.stack([x, zh, c, base]).astype(jnp.int32)
    first = absorb(scalars(HALF * c), own, o_parts)
    q_absorbed, d_out = absorb(scalars(HALF * (1 - c)), other, o_parts, first)
    return q_absorbed, d_out.transpose(0, 2, 1)


def solution(mesh):
    fine = Mesh(mesh.devices.reshape(ZL, Y, X, ZH, C), ("zl", "y", "x", "zh", "c"))
    rows = P(("zl", "y", "x", "zh", "c"), None)
    return jax.shard_map(
        on_device,
        mesh=fine,
        in_specs=(rows, rows, rows),
        out_specs=(P(("zl", "y"), None, None), P(("zl", "y"), None, BULK)),
        check_vma=False,
    )
```

time: 155 us -> 80.2 us (0.52)
  waiting for transfers between devices: 68.1 us -> 20.9 us
  starting transfers between devices: 10.6 us -> 36.7 us
  local copies, waits for them, and re-layouts: 28.8 us -> 6.16 us
  blocking collectives: 20.6 us -> 0 us
  Pallas kernels: 0 us -> 14.9 us
  between operations: 14.1 us -> 0.81 us
  matrix products: 12.1 us -> 0 us
    all_gather x2 -> x0, waiting for transfers between devices: 68.1 us -> none  [the longest x1 37.1 us: on_device(): q_all = lax.all_gather(q_part.reshape(n_fsdp * q_rows, -1), 'bulk', axis=0)]
    ppermute x0 -> x13, starting transfers between devices: none -> 27.1 us  [on_device(): over = lambda a, *d: lax.ppermute(a, BULK, shifts(*d))]
    all_to_all x2 -> x0, blocking collectives: 20.6 us -> none  [the longest x1 12 us: on_device(): lax.all_to_all(kv_send, 'fsdp', split_axis=0, concat_axis=0, tiled=True)]
    pallas_call x0 -> x2, Pallas kernels: none -> 14.9 us  [absorb(): pl.pallas_call(absorb_kernel, grid_spec=pltpu.PrefetchScalarGridSpec(num_...]
    ppermute x0 -> x13, waiting for transfers between devices: none -> 14.3 us  [on_device(): over = lambda a, *d: lax.ppermute(a, BULK, shifts(*d))]
    reshape x6 -> x3, local copies, waits for them, and re-layouts: 14.3 us -> 1.22 us  [the longest x1 1.06 us: on_device(): kv = kv_up.reshape(4, F * C, 2, HALF * NOPE).transpose(1, 2, 0, 3)]
    dot_general x2 -> x0, matrix products: 12.1 us -> none  [the longest x1 7.87 us: on_device(): jnp.einsum('rhn,lhn->hrl', query, latent[:, :, :NOPE], preferred_element_...]
    all_to_all x1, waiting for transfers between devices: 0.01 us -> 6.63 us  [on_device(): lax.all_to_all(send, ('zl', 'y', 'zh', 'c'), split_axis=0, concat_axis=0,...]
  transfers between devices with their start and end apart: 3 -> 14, of which waited for: 2 -> 4; matrix products, arithmetic and copies ran while one was open for 12% -> 4% of each run, Pallas kernels for 0% -> 9%
where the time goes in v2:
time: 80.2 us; the launch traced here: 79.9 us
  starting transfers between devices  36.7 us (46%)
  waiting for transfers between devices  20.9 us (26%)
  Pallas kernels  14.9 us (19%)
  local copies, waits for them, and re-layouts  6.16 us (8%)
  between operations  0.81 us (1%)
    ppermute x13, starting transfers between devices, on_device(): over = lambda a, *d: lax.ppermute(a, BULK, shifts(*d))  27.1 us
    pallas_call x2, Pallas kernels, absorb(): pl.pallas_call(absorb_kernel, grid_spec=pltpu.PrefetchScalarGridSpec(num_...  14.9 us
    ppermute x13, waiting for transfers between devices, on_device(): over = lambda a, *d: lax.ppermute(a, BULK, shifts(*d))  14.3 us
    all_to_all x1, starting transfers between devices, on_device(): lax.all_to_all(send, ('zl', 'y', 'zh', 'c'), split_axis=0, concat_axis=0,...  9.6 us
    all_to_all x1, waiting for transfers between devices, on_device(): lax.all_to_all(send, ('zl', 'y', 'zh', 'c'), split_axis=0, concat_axis=0,...  6.63 us
    another operation x1, local copies, waits for them, and re-layouts, on_device(): o_x = jnp.stack([o_x[d] for d in range(X)])  2.04 us
  transfers between devices with their start and end apart: 14, of which 4 were waited for; matrix products, arithmetic and copies ran while one was open for 4% of the time, Pallas kernels for 9%

profile of v2, /device:TPU:1, one launch (start us, length us, event | category | flops | bytes accessed | tf_op | source)
XLA Modules:
  0.0 79.9 jit_solution(12734585479532092285)
XLA Ops:
  0.6 1.1 %reshape.25 = bf16[4,16,2,512]{3,2,1,0:T(2,128)(2,1)S(1)} reshape(bf16[4,16384]{1,0:T(4,128)(2,1)} %param.4) | data formatting | bytes 262144 | tf_op jit(solution)/shard_map/reshape | solution.py:125
  1.7 1.0 %copy.14 = bf16[2,8,16,512]{3,2,1,0:T(8,128)(2,1)S(1)} copy(bf16[2,8,16,512]{3,1,2,0:T(8,128)(2,1)} %bitcast.30) | data formatting | bytes 524288
  2.8 0.3 copy.13
  3.1 1.0 %broadcast_in_dim.8 = bf16[8,2,2,5,4,512]{5,4,3,2,1,0:T(4,128)(2,1)} broadcast(bf16[8,2,5,4,512]{4,3,2,1,0:T(4,128)(2,1)S(1)} %bitcast.26), dimensions={0,2,3,4,5} | broadcast | bytes 983040 | tf_op jit(solution)/shard_map/broadcast_in_dim | solution.py:127
  4.1 9.6 %all-to-all-start = ((bf16[32,5,4,512]{3,2,1,0:T(4,128)(2,1)}), bf16[32,5,4,512]{3,2,1,0:T(4,128)(2,1)S(1)}, u32[]{:S(2)}, u32[]{:S(2)}) async-start(bf16[32,5,4,512]{3,2,1,0:T(4,128)(2,1)} %bitcast.7), calls=%async_computation | async-start | bytes 1310720 | tf_op jit(solution)/shard_map/all_to_all | solution.py:128
  13.8 2.0 %dynamic-slice_bitcast_fusion = (bf16[1,64,1792]{2,1,0:T(8,128)(2,1)S(1)}, bf16[64,1792]{1,0:T(8,128)(2,1)}, bf16[64,1792]{1,0:T(8,128)(2,1)S(1)}, bf16[64,1792]{1,0:T(8,128)(2,1)S(1)}) fusion(bf16[64,7168]{1,0:T(8,128)(2,1)} %param.5, s32[]{:T(128)S(6)} %select_n.18, s32[]{:T(128)S(6)} %select_n.19, s32[]{:T(128)S(6)} %select_n.21, s32[]{:T(128)S(6)} %select_n.20), kind=kLoop, calls=%fused_computation.3 | loop fusion | bytes 1835024 | tf_op jit(solution)/shard_map/stack | solution.py:137
  15.8 1.2 %collective-permute-start.7 = (bf16[64,1792]{1,0:T(8,128)(2,1)}, bf16[64,1792]{1,0:T(8,128)(2,1)S(1)}, u32[]{:S(2)}, u32[]{:S(2)}) collective-permute-start(bf16[64,1792]{1,0:T(8,128)(2,1)} %get-tuple-element.15), channel_id=1, source_target_pairs={{0,4},{1,5},{2,6},{3,7},{4,8},{5,9},{6,10},{7,11},{8,12},{9,13},{1... | collective-permute-start | bytes 688136 | tf_op jit(solution)/shard_map/ppermute | solution.py:117
  17.0 1.5 %collective-permute-start.9 = (bf16[64,1792]{1,0:T(8,128)(2,1)S(1)}, bf16[64,1792]{1,0:T(8,128)(2,1)S(1)}, u32[]{:S(2)}, u32[]{:S(2)}) collective-permute-start(bf16[64,1792]{1,0:T(8,128)(2,1)S(1)} %get-tuple-element.16), channel_id=1, source_target_pairs={{0,12},{1,13},{2,14},{3,15},{4,0},{5,1},{6,2},{7,3},{8,4},{9,5},{1... | collective-permute-start | bytes 688136 | tf_op jit(solution)/shard_map/ppermute | solution.py:117
  18.5 1.5 %collective-permute-start.8 = (bf16[64,1792]{1,0:T(8,128)(2,1)S(1)}, bf16[64,1792]{1,0:T(8,128)(2,1)S(1)}, u32[]{:S(2)}, u32[]{:S(2)}) collective-permute-start(bf16[64,1792]{1,0:T(8,128)(2,1)S(1)} %get-tuple-element.17), channel_id=1, source_target_pairs={{0,8},{1,9},{2,10},{3,11},{4,12},{5,13},{6,14},{7,15},{8,0},{9,1},... | collective-permute-start | bytes 688136 | tf_op jit(solution)/shard_map/ppermute | solution.py:117
  20.0 6.6 %all-to-all-done = bf16[32,5,4,512]{3,2,1,0:T(4,128)(2,1)S(1)} async-done(((bf16[32,5,4,512]{3,2,1,0:T(4,128)(2,1)}), bf16[32,5,4,512]{3,2,1,0:T(4,128)(2,1)S(1)}, u32[]{:S(2)}, u32[]{:S(2)}) %all-to-all-start) | async-done | bytes 655392 | tf_op jit(solution)/shard_map/all_to_all | solution.py:128
  26.6 0.1 slice_bitcast_fusion
  26.7 0.2 slice.8
  26.9 0.1 reshape.28
  27.0 0.1 copy.12
  27.1 0.1 reshape.29
  27.3 2.5 %collective-permute-start.5 = (bf16[8,80,512]{2,1,0:T(8,128)(2,1)S(1)}, bf16[8,80,512]{2,1,0:T(8,128)(2,1)}, u32[]{:S(2)}, u32[]{:S(2)}) collective-permute-start(bf16[8,80,512]{2,1,0:T(8,128)(2,1)S(1)} %constant_dynamic-update-slice_fusion.refs_0_), channel_id=1, source_target_pairs={{0,12},{1,13},{2,14},{3,15},{4,0},{5,1},{6,2},{7,3},{8,4},{9,5},{1... | collective-permute-start | bytes 1966088 | tf_op jit(solution)/shard_map/ppermute | solution.py:117
  29.8 0.5 collective-permute-start.3
  30.3 0.6 collective-permute-start.1
  31.0 0.1 pad_maximum_fusion
  31.1 0.1 constant_dynamic-slice_fusion
  31.2 2.0 %collective-permute-start.10 = (bf16[4,64,896]{2,1,0:T(8,128)(2,1)S(1)}, bf16[4,64,896]{2,1,0:T(8,128)(2,1)S(1)}, u32[]{:S(2)}, u32[]{:S(2)}) collective-permute-start(bf16[4,64,896]{2,1,0:T(8,128)(2,1)S(1)} %get-tuple-element.12), channel_id=1, source_target_pairs={{0,2},{1,3},{2,0},{3,1},{4,6},{5,7},{6,4},{7,5},{8,10},{9,11},{10,... | collective-permute-start | bytes 1376264 | tf_op jit(solution)/shard_map/ppermute | solution.py:117
  33.2 1.5 %collective-permute-start.11 = (bf16[4,64,896]{2,1,0:T(8,128)(2,1)S(1)}, bf16[4,64,896]{2,1,0:T(8,128)(2,1)S(1)}, u32[]{:S(2)}, u32[]{:S(2)}) collective-permute-start(bf16[4,64,896]{2,1,0:T(8,128)(2,1)S(1)} %get-tuple-element.13.refs_4_), channel_id=1, source_target_pairs={{0,1},{1,0},{2,3},{3,2},{4,5},{5,4},{6,7},{7,6},{8,9},{9,8},{10,11... | collective-permute-start | bytes 1376264 | tf_op jit(solution)/shard_map/ppermute | solution.py:117
  34.6 8.9 %collective-permute-done.10.refs_5_ = bf16[4,64,896]{2,1,0:T(8,128)(2,1)S(1)} collective-permute-done((bf16[4,64,896]{2,1,0:T(8,128)(2,1)S(1)}, bf16[4,64,896]{2,1,0:T(8,128)(2,1)S(1)}, u32[]{:S(2)}, u32[]{:S(2)}) %collective-permute-start.10) | collective-permute-done | bytes 458784 | tf_op jit(solution)/shard_map/ppermute | solution.py:117
  43.5 2.2 %collective-permute-start = (bf16[8,80,512]{2,1,0:T(8,128)(2,1)S(1)}, bf16[8,80,512]{2,1,0:T(8,128)(2,1)S(1)}, u32[]{:S(2)}, u32[]{:S(2)}) collective-permute-start(bf16[8,80,512]{2,1,0:T(8,128)(2,1)S(1)} %constant_dynamic-update-slice_fusion.refs_0_), channel_id=1, source_target_pairs={{0,1},{1,0},{2,3},{3,2},{4,5},{5,4},{6,7},{7,6},{8,9},{9,8},{10,11... | collective-permute-start | bytes 1966088 | tf_op jit(solution)/shard_map/ppermute | solution.py:117
  45.7 13.1 %collective-permute-start.6 = (bf16[8,80,512]{2,1,0:T(8,128)(2,1)}, bf16[8,80,512]{2,1,0:T(8,128)(2,1)}, u32[]{:S(2)}, u32[]{:S(2)}) collective-permute-start(bf16[8,80,512]{2,1,0:T(8,128)(2,1)} %collective-permute-done.5.refs_3_), channel_id=1, source_target_pairs={{0,1},{1,0},{2,3},{3,2},{4,5},{5,4},{6,7},{7,6},{8,9},{9,8},{10,11... | collective-permute-start | bytes 1966088 | tf_op jit(solution)/shard_map/ppermute | solution.py:117
  58.8 3.3 %collective-permute-done.1.refs_1_ = bf16[8,80,512]{2,1,0:T(8,128)(2,1)} collective-permute-done((bf16[8,80,512]{2,1,0:T(8,128)(2,1)S(1)}, bf16[8,80,512]{2,1,0:T(8,128)(2,1)}, u32[]{:S(2)}, u32[]{:S(2)}) %collective-permute-start.1) | collective-permute-done | bytes 655392 | tf_op jit(solution)/shard_map/ppermute | solution.py:117
  62.1 0.5 collective-permute-start.2
  62.6 0.1 pad_add_fusion.2
  62.7 0.1 pad_add_fusion.s_ref
  62.8 2.1 %collective-permute-done.12.refs_7_ = bf16[4,64,896]{2,1,0:T(8,128)(2,1)S(1)} collective-permute-done((bf16[4,64,896]{2,1,0:T(8,128)(2,1)S(1)}, bf16[4,64,896]{2,1,0:T(8,128)(2,1)S(1)}, u32[]{:S(2)}, u32[]{:S(2)}) %collective-permute-start.12) | collective-permute-done | bytes 458784 | tf_op jit(solution)/shard_map/ppermute | solution.py:117
  64.9 7.5 %shard_map.50 = (bf16[8,1536,512]{2,1,0:T(8,128)(2,1)}, bf16[8,448,512]{2,1,0:T(8,128)(2,1)}) custom-call(s32[4]{0:T(128)S(1)} %get-tuple-element.10.s_ref, bf16[8,80,512]{2,1,0:T(8,128)(2,1)S(1)} %constant_dynamic-update-slice_fusion.refs_0_, bf16[8,80,512]{2,1,0:T(8,128)(2,1)} %collective-permute-done.1.refs_1_, ...), custom_call_target="tpu_custom_call" | custom-call | flops 1073741824 | bytes 10747904 | tf_op jit(solution)/shard_map/pallas_call | solution.py:89
  72.4 7.5 %shard_map.51 = (bf16[8,1536,512]{2,1,0:T(8,128)(2,1)}, bf16[8,448,512]{2,1,0:T(8,128)(2,1)}) custom-call(s32[4]{0:T(128)S(1)} %pad_add_fusion.s_ref, bf16[8,80,512]{2,1,0:T(8,128)(2,1)S(1)} %collective-permute-done.refs_0_, bf16[8,80,512]{2,1,0:T(8,128)(2,1)} %collective-permute-done.2.refs_1_, ...), custom_call_target="tpu_custom_call", output_to_operand_aliasing={{0}: (9, {}), {1}: (10, {})} | custom-call | flops 1073741824 | bytes 10747904 | tf_op jit(solution)/shard_map/pallas_call | solution.py:89
  (17 shorter events, 0.2 us)
Async XLA Ops:
  4.1 22.5 %all-to-all-start = ((bf16[32,5,4,512]{3,2,1,0:T(4,128)(2,1)}), bf16[32,5,4,512]{3,2,1,0:T(4,128)(2,1)S(1)}, u32[]{:S(2)}, u32[]{:S(2)}) async-start(bf16[32,5,4,512]{3,2,1,0:T(4,128)(2,1)} %bitcast.7), calls=%async_computation | async-start | bytes 1310720 | tf_op jit(solution)/shard_map/all_to_all | solution.py:128
  15.8 14.5 %collective-permute-start.7 = (bf16[64,1792]{1,0:T(8,128)(2,1)}, bf16[64,1792]{1,0:T(8,128)(2,1)S(1)}, u32[]{:S(2)}, u32[]{:S(2)}) collective-permute-start(bf16[64,1792]{1,0:T(8,128)(2,1)} %get-tuple-element.15), channel_id=1, source_target_pairs={{0,4},{1,5},{2,6},{3,7},{4,8},{5,9},{6,10},{7,11},{8,12},{9,13},{1... | collective-permute-start | bytes 688136 | tf_op jit(solution)/shard_map/ppermute | solution.py:117
  17.0 13.9 %collective-permute-start.9 = (bf16[64,1792]{1,0:T(8,128)(2,1)S(1)}, bf16[64,1792]{1,0:T(8,128)(2,1)S(1)}, u32[]{:S(2)}, u32[]{:S(2)}) collective-permute-start(bf16[64,1792]{1,0:T(8,128)(2,1)S(1)} %get-tuple-element.16), channel_id=1, source_target_pairs={{0,12},{1,13},{2,14},{3,15},{4,0},{5,1},{6,2},{7,3},{8,4},{9,5},{1... | collective-permute-start | bytes 688136 | tf_op jit(solution)/shard_map/ppermute | solution.py:117
  18.5 12.5 %collective-permute-start.8 = (bf16[64,1792]{1,0:T(8,128)(2,1)S(1)}, bf16[64,1792]{1,0:T(8,128)(2,1)S(1)}, u32[]{:S(2)}, u32[]{:S(2)}) collective-permute-start(bf16[64,1792]{1,0:T(8,128)(2,1)S(1)} %get-tuple-element.17), channel_id=1, source_target_pairs={{0,8},{1,9},{2,10},{3,11},{4,12},{5,13},{6,14},{7,15},{8,0},{9,1},... | collective-permute-start | bytes 688136 | tf_op jit(solution)/shard_map/ppermute | solution.py:117
  27.3 18.5 %collective-permute-start.5 = (bf16[8,80,512]{2,1,0:T(8,128)(2,1)S(1)}, bf16[8,80,512]{2,1,0:T(8,128)(2,1)}, u32[]{:S(2)}, u32[]{:S(2)}) collective-permute-start(bf16[8,80,512]{2,1,0:T(8,128)(2,1)S(1)} %constant_dynamic-update-slice_fusion.refs_0_), channel_id=1, source_target_pairs={{0,12},{1,13},{2,14},{3,15},{4,0},{5,1},{6,2},{7,3},{8,4},{9,5},{1... | collective-permute-start | bytes 1966088 | tf_op jit(solution)/shard_map/ppermute | solution.py:117
  29.8 29.0 %collective-permute-start.3 = (bf16[8,80,512]{2,1,0:T(8,128)(2,1)S(1)}, bf16[8,80,512]{2,1,0:T(8,128)(2,1)}, u32[]{:S(2)}, u32[]{:S(2)}) collective-permute-start(bf16[8,80,512]{2,1,0:T(8,128)(2,1)S(1)} %constant_dynamic-update-slice_fusion.refs_0_), channel_id=1, source_target_pairs={{0,8},{1,9},{2,10},{3,11},{4,12},{5,13},{6,14},{7,15},{8,0},{9,1},... | collective-permute-start | bytes 1966088 | tf_op jit(solution)/shard_map/ppermute | solution.py:117
  30.3 31.8 %collective-permute-start.1 = (bf16[8,80,512]{2,1,0:T(8,128)(2,1)S(1)}, bf16[8,80,512]{2,1,0:T(8,128)(2,1)}, u32[]{:S(2)}, u32[]{:S(2)}) collective-permute-start(bf16[8,80,512]{2,1,0:T(8,128)(2,1)S(1)} %constant_dynamic-update-slice_fusion.refs_0_), channel_id=1, source_target_pairs={{0,4},{1,5},{2,6},{3,7},{4,8},{5,9},{6,10},{7,11},{8,12},{9,13},{1... | collective-permute-start | bytes 1966088 | tf_op jit(solution)/shard_map/ppermute | solution.py:117
  31.2 12.3 %collective-permute-start.10 = (bf16[4,64,896]{2,1,0:T(8,128)(2,1)S(1)}, bf16[4,64,896]{2,1,0:T(8,128)(2,1)S(1)}, u32[]{:S(2)}, u32[]{:S(2)}) collective-permute-start(bf16[4,64,896]{2,1,0:T(8,128)(2,1)S(1)} %get-tuple-element.12), channel_id=1, source_target_pairs={{0,2},{1,3},{2,0},{3,1},{4,6},{5,7},{6,4},{7,5},{8,10},{9,11},{10,... | collective-permute-start | bytes 1376264 | tf_op jit(solution)/shard_map/ppermute | solution.py:117
  33.2 29.4 %collective-permute-start.11 = (bf16[4,64,896]{2,1,0:T(8,128)(2,1)S(1)}, bf16[4,64,896]{2,1,0:T(8,128)(2,1)S(1)}, u32[]{:S(2)}, u32[]{:S(2)}) collective-permute-start(bf16[4,64,896]{2,1,0:T(8,128)(2,1)S(1)} %get-tuple-element.13.refs_4_), channel_id=1, source_target_pairs={{0,1},{1,0},{2,3},{3,2},{4,5},{5,4},{6,7},{7,6},{8,9},{9,8},{10,11... | collective-permute-start | bytes 1376264 | tf_op jit(solution)/shard_map/ppermute | solution.py:117
  43.5 28.9 %collective-permute-start = (bf16[8,80,512]{2,1,0:T(8,128)(2,1)S(1)}, bf16[8,80,512]{2,1,0:T(8,128)(2,1)S(1)}, u32[]{:S(2)}, u32[]{:S(2)}) collective-permute-start(bf16[8,80,512]{2,1,0:T(8,128)(2,1)S(1)} %constant_dynamic-update-slice_fusion.refs_0_), channel_id=1, source_target_pairs={{0,1},{1,0},{2,3},{3,2},{4,5},{5,4},{6,7},{7,6},{8,9},{9,8},{10,11... | collective-permute-start | bytes 1966088 | tf_op jit(solution)/shard_map/ppermute | solution.py:117
  45.7 26.7 %collective-permute-start.6 = (bf16[8,80,512]{2,1,0:T(8,128)(2,1)}, bf16[8,80,512]{2,1,0:T(8,128)(2,1)}, u32[]{:S(2)}, u32[]{:S(2)}) collective-permute-start(bf16[8,80,512]{2,1,0:T(8,128)(2,1)} %collective-permute-done.5.refs_3_), channel_id=1, source_target_pairs={{0,1},{1,0},{2,3},{3,2},{4,5},{5,4},{6,7},{7,6},{8,9},{9,8},{10,11... | collective-permute-start | bytes 1966088 | tf_op jit(solution)/shard_map/ppermute | solution.py:117
  58.8 13.6 %collective-permute-start.4 = (bf16[8,80,512]{2,1,0:T(8,128)(2,1)}, bf16[8,80,512]{2,1,0:T(8,128)(2,1)}, u32[]{:S(2)}, u32[]{:S(2)}) collective-permute-start(bf16[8,80,512]{2,1,0:T(8,128)(2,1)} %collective-permute-done.3.refs_2_), channel_id=1, source_target_pairs={{0,1},{1,0},{2,3},{3,2},{4,5},{5,4},{6,7},{7,6},{8,9},{9,8},{10,11... | collective-permute-start | bytes 1966088 | tf_op jit(solution)/shard_map/ppermute | solution.py:117
  62.1 10.3 %collective-permute-start.2 = (bf16[8,80,512]{2,1,0:T(8,128)(2,1)}, bf16[8,80,512]{2,1,0:T(8,128)(2,1)}, u32[]{:S(2)}, u32[]{:S(2)}) collective-permute-start(bf16[8,80,512]{2,1,0:T(8,128)(2,1)} %collective-permute-done.1.refs_1_), channel_id=1, source_target_pairs={{0,1},{1,0},{2,3},{3,2},{4,5},{5,4},{6,7},{7,6},{8,9},{9,8},{10,11... | collective-permute-start | bytes 1966088 | tf_op jit(solution)/shard_map/ppermute | solution.py:117
  62.6 2.3 %collective-permute-start.12 = (bf16[4,64,896]{2,1,0:T(8,128)(2,1)S(1)}, bf16[4,64,896]{2,1,0:T(8,128)(2,1)S(1)}, u32[]{:S(2)}, u32[]{:S(2)}) collective-permute-start(bf16[4,64,896]{2,1,0:T(8,128)(2,1)S(1)} %collective-permute-done.10.refs_5_), channel_id=1, source_target_pairs={{0,1},{1,0},{2,3},{3,2},{4,5},{5,4},{6,7},{7,6},{8,9},{9,8},{10,11... | collective-permute-start | bytes 1376264 | tf_op jit(solution)/shard_map/ppermute | solution.py:117

commit v3 on v1

v3 whole, which is shorter than its diff:
```python
import functools

import jax
import jax.numpy as jnp
from jax import lax
from jax.experimental import pallas as pl
from jax.experimental.pallas import tpu as pltpu
from jax.sharding import Mesh, PartitionSpec as P

QL = 1536
KVL = 512
NOPE = 128
VD = 128
X, ZH, ZL, Y, C = 4, 2, 2, 4, 2
BULK = ("x", "zh", "c")
OWNERS = ("zl", "y", "zh", "c")
F = ZL * Y
HEADS = 8
HALF = 4
WIDE = HALF * NOPE
Q_ROWS, KV_ROWS = 12, 4
Q_BLOCK = ZH * C * Q_ROWS
Q_ALL = F * Q_BLOCK
L_BLOCK = ZH * C * KV_ROWS
SPLIT = (Q_ALL + 2 * F * L_BLOCK) // 2
D_PART = 448
bf16 = jnp.bfloat16
PACK_MIB = 56
VMEM = pl.BlockSpec(memory_space=pltpu.VMEM)
ANY = pl.BlockSpec(memory_space=pl.ANY)


def shifts(dx, dz, dc):
    at = lambda x, z, c: (x * ZH + z) * C + c
    return [
        (at(x, z, c), at((x + dx) % X, (z + dz) % ZH, (c + dc) % C))
        for x in range(X)
        for z in range(ZH)
        for c in range(C)
    ]


COST = pl.CostEstimate(flops=1024, bytes_accessed=1024, transcendentals=0)


def limit(mib):
    return pltpu.CompilerParams(vmem_limit_bytes=mib * 2**20)


def pack_kernel(q_hbm, kv_hbm, o_hbm, out_ref, *refs):
    o_refs, (q_ref, kv_ref, sems) = refs[:X], refs[X:]
    kv_copy = pltpu.make_async_copy(kv_hbm, kv_ref, sems.at[0])
    q_copy = pltpu.make_async_copy(q_hbm, q_ref, sems.at[1])
    kv_copy.start()
    q_copy.start()
    copies = []
    o_cols = o_hbm.shape[1] // X
    for d in range(X):
        at = pl.multiple_of(lax.rem(lax.axis_index("x") + d, X) * o_cols, 128)
        copies.append(
            pltpu.make_async_copy(o_hbm.at[:, pl.ds(at, o_cols)], o_refs[d], sems.at[2 + d])
        )
        copies[d].start()
    kv_copy.wait()
    for n in range(F * C):
        for z in range(ZH):
            at = (n // C * ZH + z) * C + n % C
            out_ref[at, Q_ROWS:, :WIDE] = kv_ref[:, n * 1024 : n * 1024 + WIDE]
            for j in range(4):
                lane = n * 1024 + WIDE + j * 128
                out_ref[at, j * 4 : (j + 1) * 4, WIDE:] = kv_ref[:, lane : lane + 128]
    q_copy.wait()
    for n in range(F * C):
        for z in range(ZH):
            at = (n // C * ZH + z) * C + n % C
            out_ref[at, :Q_ROWS, :WIDE] = q_ref[:, n * WIDE : (n + 1) * WIDE]
    for copy in copies:
        copy.wait()


def pack(q, kv, o):
    o_cols = o.shape[1] // X
    out = pl.pallas_call(
        pack_kernel,
        in_specs=[ANY] * 3,
        out_specs=[VMEM] * (X + 1),
        out_shape=[jax.ShapeDtypeStruct((F * ZH * C, 16, 640), bf16)]
        + [jax.ShapeDtypeStruct((o.shape[0], o_cols), bf16)] * X,
        scratch_shapes=[
            pltpu.VMEM(q.shape, bf16),
            pltpu.VMEM(kv.shape, bf16),
            pltpu.SemaphoreType.DMA((2 + X,)),
        ],
        compiler_params=limit(PACK_MIB),
        cost_estimate=COST,
    )(q, kv, o)
    return out[0], out[1:]


def unpack_kernel(packed_ref, left_ref, right_ref, first, second):
    half_q, half_l = F // 2 * Q_BLOCK, F // 2 * L_BLOCK

    def put(at, block):
        cut = max(0, min(block.shape[0], SPLIT - at))
        if cut:
            first[at : at + cut, : block.shape[1]] = block[:cut]
        if cut < block.shape[0]:
            second[at + cut - SPLIT : at + block.shape[0] - SPLIT] = block[cut:]

    for g in range(2):
        packed = packed_ref[g * 256 : (g + 1) * 256]
        left = jnp.dot(left_ref[...], packed[:, :WIDE], preferred_element_type=jnp.float32)
        right = jnp.dot(right_ref[...], packed[:, WIDE:], preferred_element_type=jnp.float32)
        left, right = left.astype(bf16), right.astype(bf16)
        put(g * half_q, left[:half_q])
        put(Q_ALL + g * half_l, left[half_q:])
        at = Q_ALL + g * half_l + F * L_BLOCK
        lanes = [right[j * half_l : (j + 1) * half_l] for j in range(4)]
        put(at, jnp.concatenate(lanes, axis=1))


def unpack(packed):
    row, column = jnp.arange(256), jnp.arange(256)[None, :]
    of_q = row // Q_ROWS * 16 + row % Q_ROWS
    r = row % 64
    of_kv = r // KV_ROWS * 16 + r % KV_ROWS
    left = jnp.where(row < 192, of_q, of_kv + Q_ROWS)
    right = of_kv + row // 64 * 4
    select = lambda source: (source[:, None] == column).astype(bf16)
    return pl.pallas_call(
        unpack_kernel,
        out_shape=[jax.ShapeDtypeStruct((SPLIT, WIDE), bf16)] * 2,
        compiler_params=limit(8),
        cost_estimate=COST,
    )(packed, select(left), select(right))


def sort_kernel(*refs):
    parts, out, kv = refs[: 2 * X], refs[2 * X], refs[2 * X + 1]
    for d in range(X):
        first, second = parts[2 * d], parts[2 * d + 1]
        xs = lax.rem(lax.axis_index("x") - d + X, X)
        for f in range(F):
            at = pl.multiple_of(f * (X * L_BLOCK) + xs * L_BLOCK, L_BLOCK)
            for h in range(2):
                source = Q_ALL + (h * F + f) * L_BLOCK - SPLIT
                rows = second[source : source + L_BLOCK]
                kv[pl.ds(at, L_BLOCK), h * WIDE : (h + 1) * WIDE] = rows
        at = 2 * KVL + d * Q_ALL
        out[at : at + SPLIT] = first[...]
        out[at + SPLIT : at + Q_ALL] = second[: Q_ALL - SPLIT]
    for k in range(HALF):
        out[k * NOPE : (k + 1) * NOPE] = kv[:, k * 256 : k * 256 + NOPE].T
        out[KVL : 2 * KVL, k * VD : (k + 1) * VD] = kv[:, k * 256 + NOPE : (k + 1) * 256]


def sort_rows(parts):
    return pl.pallas_call(
        sort_kernel,
        in_specs=[VMEM] * (2 * X),
        out_specs=VMEM,
        out_shape=jax.ShapeDtypeStruct((2 * KVL + X * Q_ALL, WIDE), bf16),
        scratch_shapes=[pltpu.VMEM((KVL, 1024), bf16)],
        compiler_params=limit(12),
        cost_estimate=COST,
    )(*parts)


def sender(sems):
    copies = []

    def send(source, target):
        copy = pltpu.make_async_copy(source, target, sems.at[len(copies)])
        copy.start()
        copies.append(copy)

    return copies, send


def query_blocks(x, half, rows_ref, q_out, blocks, send):
    for d in range(X):
        xs = lax.rem(x - d + X, X)
        first = 2 * KVL + d * Q_ALL
        for k in range(HALF):
            lanes = slice(k * NOPE, (k + 1) * NOPE)
            block = jnp.dot(
                rows_ref[first : first + Q_ALL, lanes],
                rows_ref[lanes],
                preferred_element_type=jnp.float32,
            )
            at = d * HALF + k
            blocks[at] = block.astype(bf16).reshape(F, Q_BLOCK, KVL)
            send(blocks.at[at], q_out.at[half * HALF + k, :, xs])


def absorb_kernel(mine, *refs):
    rows_ref, own_refs, other_refs = refs[0], refs[1:3], refs[3:5]
    q_out, d_out, blocks, heads, wide, sems = refs[-6:]
    x, zh, c = (lax.axis_index(a) for a in BULK)
    half = c if mine else 1 - c
    copies, send = sender(sems)
    query_blocks(x, half, rows_ref, q_out, blocks, send)
    lanes = pl.ds(pl.multiple_of(c * 384, 128), 512)
    own_at = pl.ds(pl.multiple_of(c * 64, 64), 64)
    other_at = pl.ds(pl.multiple_of((1 - c) * 64, 64), 64)
    part = pl.ds(pl.multiple_of(c * 64, 64), D_PART)
    for k in range(HALF):
        d = lax.rem(x - (2 * half + k // 2) + X, X)
        for z in range(ZH):

            @pl.when(lax.rem(zh + k, ZH) == z)
            def _():
                heads[k, own_at, :] = own_refs[z][d, :, lanes]
                heads[k, other_at, :] = other_refs[z][d, :, lanes]

    for k in range(HALF):
        value = rows_ref[KVL : 2 * KVL, k * VD : (k + 1) * VD]
        wide[k] = lax.dot_general(
            heads[k], value, (((0,), (1,)), ((), ())), preferred_element_type=jnp.float32
        ).astype(bf16)
        send(wide.at[k, part], d_out.at[half * HALF + k])
    for copy in copies:
        copy.wait()


def absorb(mine, rows, o_own, o_other, earlier=()):
    return pl.pallas_call(
        functools.partial(absorb_kernel, mine),
        in_specs=[VMEM] * 5 + [ANY] * len(earlier),
        out_specs=[ANY, ANY],
        scratch_shapes=[
            pltpu.VMEM((X * HALF, F, Q_BLOCK, KVL), bf16),
            pltpu.VMEM((HALF, VD, 512), bf16),
            pltpu.VMEM((HALF, 512, KVL), bf16),
            pltpu.SemaphoreType.DMA((X * HALF + HALF,)),
        ],
        out_shape=[
            jax.ShapeDtypeStruct((HEADS, F, X, Q_BLOCK, KVL), bf16),
            jax.ShapeDtypeStruct((HEADS, D_PART, KVL), bf16),
        ],
        input_output_aliases={5: 0, 6: 1} if earlier else {},
        compiler_params=limit(20),
        cost_estimate=COST,
    )(rows, *o_own, *o_other, *earlier)


def on_device(q_nope, kv_up, o_proj):
    zh = lax.axis_index("zh")
    over = lambda a, *d: lax.ppermute(a, BULK, shifts(*d))
    core = (0, 0, 1)

    packed, o_send = pack(q_nope, kv_up, o_proj)
    packed = lax.all_to_all(packed, OWNERS, split_axis=0, concat_axis=0, tiled=True)
    o_x = [o_send[0]] + [over(o_send[d], d, 0, 0) for d in (1, 2, 3)]
    packed, o_x = lax.optimization_barrier((packed, o_x))

    right, left = (1, 0, 0), (3, 0, 0)
    own = unpack(packed.reshape(F * ZH * C * 16, 640))
    from_left, from_right = [over(own[0], *right)], [over(own[1], *left)]
    from_left.append(over(own[1], *right))
    from_right.insert(0, over(own[0], *left))
    far = [over(from_left[0], *right), over(from_right[1], *left)]
    o_x = jnp.stack(o_x)
    half = lambda z: lax.dynamic_slice_in_dim(o_x, z * (2 * D_PART), 2 * D_PART, 2)
    o_own = [half(zh), over(half(1 - zh), 0, 1, 0)]
    o_other = [over(o, *core) for o in o_own]
    arrived = [*from_left, *far, *from_right]
    arrived, o_own, o_other = lax.optimization_barrier((arrived, o_own, o_other))

    rows = sort_rows([*own, *arrived])
    rows_other = over(rows, *core)
    outs = absorb(True, rows, o_own, o_other)
    q_out, d_out = absorb(False, rows_other, o_own, o_other, outs)
    return q_out.reshape(HEADS, QL, KVL), d_out.transpose(0, 2, 1)


def solution(mesh):
    fine = Mesh(mesh.devices.reshape(ZL, Y, X, ZH, C), ("zl", "y", "x", "zh", "c"))
    rows = P(("zl", "y", "x", "zh", "c"), None)
    return jax.shard_map(
        on_device,
        mesh=fine,
        in_specs=(rows, rows, rows),
        out_specs=(P(("zl", "y"), None, None), P(("zl", "y"), None, BULK)),
        check_vma=False,
    )
```

time: 155 us -> 70.2 us (0.45)
  waiting for transfers between devices: 68.1 us -> 23.6 us
  local copies, waits for them, and re-layouts: 28.8 us -> 0.13 us
  starting transfers between devices: 10.6 us -> 33.7 us
  blocking collectives: 20.6 us -> 0 us
  between operations: 14.1 us -> 0.7 us
  matrix products: 12.1 us -> 0 us
  Pallas kernels: 0 us -> 10.6 us
    all_gather x2 -> x0, waiting for transfers between devices: 68.1 us -> none  [the longest x1 37.1 us: on_device(): q_all = lax.all_gather(q_part.reshape(n_fsdp * q_rows, -1), 'bulk', axis=0)]
    ppermute x0 -> x13, starting transfers between devices: none -> 24.1 us  [on_device(): over = lambda a, *d: lax.ppermute(a, BULK, shifts(*d))]
    ppermute x0 -> x13, waiting for transfers between devices: none -> 23.6 us  [on_device(): over = lambda a, *d: lax.ppermute(a, BULK, shifts(*d))]
    all_to_all x2 -> x0, blocking collectives: 20.6 us -> none  [the longest x1 12 us: on_device(): lax.all_to_all(kv_send, 'fsdp', split_axis=0, concat_axis=0, tiled=True)]
    reshape x6 -> x0, local copies, waits for them, and re-layouts: 14.3 us -> none  [the longest x1 5.56 us: on_device(): query = query.reshape(QL, heads, NOPE)]
    dot_general x2 -> x0, matrix products: 12.1 us -> none  [the longest x1 7.87 us: on_device(): jnp.einsum('rhn,lhn->hrl', query, latent[:, :, :NOPE], preferred_element_...]
    pallas_call x0 -> x5, Pallas kernels: none -> 10.6 us  [the longest x2 7.23 us: absorb(): pl.pallas_call(functools.partial(absorb_kernel, mine), in_specs=[VMEM] *...]
    transpose x1 -> x0, local copies, waits for them, and re-layouts: 4.02 us -> none  [on_device(): query = q_all.reshape(n_bulk, n_fsdp, q_rows, -1).transpose(1, 0, 2, 3)]
  transfers between devices with their start and end apart: 3 -> 14, of which waited for: 2 -> 7; matrix products, arithmetic and copies ran while one was open for 12% -> 0% of each run, Pallas kernels for 0% -> 6%
where the time goes in v3:
time: 70.2 us; the launch traced here: 69.9 us
  starting transfers between devices  33.7 us (48%)
  waiting for transfers between devices  23.6 us (34%)
  Pallas kernels  10.6 us (15%)
  other arithmetic  1.21 us (2%)
    ppermute x13, starting transfers between devices, on_device(): over = lambda a, *d: lax.ppermute(a, BULK, shifts(*d))  24.1 us
    ppermute x13, waiting for transfers between devices, on_device(): over = lambda a, *d: lax.ppermute(a, BULK, shifts(*d))  23.6 us
    all_to_all x1, starting transfers between devices, on_device(): lax.all_to_all(packed, OWNERS, split_axis=0, concat_axis=0, tiled=True)  9.61 us
    pallas_call x2, Pallas kernels, absorb(): pl.pallas_call(functools.partial(absorb_kernel, mine), in_specs=[VMEM] *...  7.23 us
    pallas_call x1, Pallas kernels, pack(): pl.pallas_call(pack_kernel, in_specs=[ANY] * 3, out_specs=[VMEM] * (X + 1...  2.54 us
  transfers between devices with their start and end apart: 14, of which 7 were waited for; matrix products, arithmetic and copies ran while one was open for 0% of the time, Pallas kernels for 6%

profile of v3, /device:TPU:1, one launch (start us, length us, event | category | flops | bytes accessed | tf_op | source)
XLA Modules:
  0.0 69.9 jit_solution(2192307204373865188)
XLA Ops:
  0.6 2.5 %shard_map.50 = (bf16[32,16,640]{2,1,0:T(8,128)(2,1)}, bf16[64,1792]{1,0:T(8,128)(2,1)}, bf16[64,1792]{1,0:T(8,128)(2,1)}, bf16[64,1792]{1,0:T(8,128)(2,1)}, bf16[64,1792]{1,0:T(8,128)(2,1)}) custom-call(bf16[12,8192]{1,0:T(8,128)(2,1)} %q_hbm.1, bf16[4,16384]{1,0:T(4,128)(2,1)} %kv_hbm.1, bf16[64,7168]{1,0:T(8,128)(2,1)} %o_hbm.1), custom_call_target="tpu_custom_call" | custom-call | flops 1024 | bytes 1024 | tf_op jit(solution)/shard_map/pallas_call | solution.py:83
  3.2 9.6 %all-to-all-start = ((bf16[32,16,640]{2,1,0:T(8,128)(2,1)}), bf16[32,16,640]{2,1,0:T(8,128)(2,1)S(1)}, u32[]{:S(2)}, u32[]{:S(2)}) async-start(bf16[32,16,640]{2,1,0:T(8,128)(2,1)} %get-tuple-element.28), calls=%async_computation | async-start | bytes 1310720 | tf_op jit(solution)/shard_map/all_to_all | solution.py:253
  12.8 1.3 %collective-permute-start = (bf16[64,1792]{1,0:T(8,128)(2,1)}, bf16[64,1792]{1,0:T(8,128)(2,1)S(1)}, u32[]{:S(2)}, u32[]{:S(2)}) collective-permute-start(bf16[64,1792]{1,0:T(8,128)(2,1)} %get-tuple-element.30), channel_id=1, source_target_pairs={{0,4},{1,5},{2,6},{3,7},{4,8},{5,9},{6,10},{7,11},{8,12},{9,13},{1... | collective-permute-start | bytes 688136 | tf_op jit(solution)/shard_map/ppermute | solution.py:249
  14.1 2.5 %collective-permute-start.1 = (bf16[64,1792]{1,0:T(8,128)(2,1)}, bf16[64,1792]{1,0:T(8,128)(2,1)S(1)}, u32[]{:S(2)}, u32[]{:S(2)}) collective-permute-start(bf16[64,1792]{1,0:T(8,128)(2,1)} %get-tuple-element.31), channel_id=1, source_target_pairs={{0,8},{1,9},{2,10},{3,11},{4,12},{5,13},{6,14},{7,15},{8,0},{9,1},... | collective-permute-start | bytes 688136 | tf_op jit(solution)/shard_map/ppermute | solution.py:249
  16.5 1.2 %collective-permute-start.2 = (bf16[64,1792]{1,0:T(8,128)(2,1)}, bf16[64,1792]{1,0:T(8,128)(2,1)S(1)}, u32[]{:S(2)}, u32[]{:S(2)}) collective-permute-start(bf16[64,1792]{1,0:T(8,128)(2,1)} %get-tuple-element.32), channel_id=1, source_target_pairs={{0,12},{1,13},{2,14},{3,15},{4,0},{5,1},{6,2},{7,3},{8,4},{9,5},{1... | collective-permute-start | bytes 688136 | tf_op jit(solution)/shard_map/ppermute | solution.py:249
  17.7 3.6 %collective-permute-done = bf16[64,1792]{1,0:T(8,128)(2,1)S(1)} collective-permute-done((bf16[64,1792]{1,0:T(8,128)(2,1)}, bf16[64,1792]{1,0:T(8,128)(2,1)S(1)}, u32[]{:S(2)}, u32[]{:S(2)}) %collective-permute-start) | collective-permute-done | bytes 229408 | tf_op jit(solution)/shard_map/ppermute | solution.py:249
  21.3 5.9 %collective-permute-done.1 = bf16[64,1792]{1,0:T(8,128)(2,1)S(1)} collective-permute-done((bf16[64,1792]{1,0:T(8,128)(2,1)}, bf16[64,1792]{1,0:T(8,128)(2,1)S(1)}, u32[]{:S(2)}, u32[]{:S(2)}) %collective-permute-start.1) | collective-permute-done | bytes 229408 | tf_op jit(solution)/shard_map/ppermute | solution.py:249
  27.2 0.0 collective-permute-done.2
  27.2 0.0 all-to-all-done
  27.2 1.1 %pad_maximum_fusion = bf16[4,64,1792]{2,1,0:T(8,128)(2,1)S(1)} fusion(bf16[1,64,1792]{2,1,0:T(8,128)(2,1)S(1)} %bitcast.13, bf16[1,64,1792]{2,1,0:T(8,128)(2,1)S(1)} %bitcast.12, bf16[1,64,1792]{2,1,0:T(8,128)(2,1)S(1)} %bitcast.11, bf16[1,64,1792]{2,1,0:T(8,128)(2,1)} %bitcast.10), kind=kLoop, calls=%fused_computation | loop fusion | flops 1376256 | bytes 1835008 | tf_op jit(solution)/shard_map/stack | solution.py:263
  28.2 0.1 constant_dynamic-slice_fusion
  28.4 2.8 %collective-permute-start.9 = (bf16[4,64,896]{2,1,0:T(8,128)(2,1)S(1)}, bf16[4,64,896]{2,1,0:T(8,128)(2,1)S(1)}, u32[]{:S(2)}, u32[]{:S(2)}) collective-permute-start(bf16[4,64,896]{2,1,0:T(8,128)(2,1)S(1)} %get-tuple-element.54), channel_id=1, source_target_pairs={{0,2},{1,3},{2,0},{3,1},{4,6},{5,7},{6,4},{7,5},{8,10},{9,11},{10,... | collective-permute-start | bytes 1376264 | tf_op jit(solution)/shard_map/ppermute | solution.py:249
  31.2 0.1 fusion
  31.3 0.4 shard_map.51
  31.7 2.7 %collective-permute-start.8 = (bf16[320,512]{1,0:T(8,128)(2,1)S(1)}, bf16[320,512]{1,0:T(8,128)(2,1)S(1)}, u32[]{:S(2)}, u32[]{:S(2)}) collective-permute-start(bf16[320,512]{1,0:T(8,128)(2,1)S(1)} %get-tuple-element.34.refs_0_), channel_id=1, source_target_pairs={{0,12},{1,13},{2,14},{3,15},{4,0},{5,1},{6,2},{7,3},{8,4},{9,5},{1... | collective-permute-start | bytes 983048 | tf_op jit(solution)/shard_map/ppermute | solution.py:249
  34.5 2.7 %collective-permute-start.6 = (bf16[320,512]{1,0:T(8,128)(2,1)S(1)}, bf16[320,512]{1,0:T(8,128)(2,1)S(1)}, u32[]{:S(2)}, u32[]{:S(2)}) collective-permute-start(bf16[320,512]{1,0:T(8,128)(2,1)S(1)} %get-tuple-element.35.refs_1_), channel_id=1, source_target_pairs={{0,12},{1,13},{2,14},{3,15},{4,0},{5,1},{6,2},{7,3},{8,4},{9,5},{1... | collective-permute-start | bytes 983048 | tf_op jit(solution)/shard_map/ppermute | solution.py:249
  37.1 1.6 %collective-permute-start.10 = (bf16[4,64,896]{2,1,0:T(8,128)(2,1)S(1)}, bf16[4,64,896]{2,1,0:T(8,128)(2,1)S(1)}, u32[]{:S(2)}, u32[]{:S(2)}) collective-permute-start(bf16[4,64,896]{2,1,0:T(8,128)(2,1)S(1)} %get-tuple-element.46.refs_1_), channel_id=1, source_target_pairs={{0,1},{1,0},{2,3},{3,2},{4,5},{5,4},{6,7},{7,6},{8,9},{9,8},{10,11... | collective-permute-start | bytes 1376264 | tf_op jit(solution)/shard_map/ppermute | solution.py:249
  38.8 2.1 %collective-permute-done.9.refs_2_ = bf16[4,64,896]{2,1,0:T(8,128)(2,1)S(1)} collective-permute-done((bf16[4,64,896]{2,1,0:T(8,128)(2,1)S(1)}, bf16[4,64,896]{2,1,0:T(8,128)(2,1)S(1)}, u32[]{:S(2)}, u32[]{:S(2)}) %collective-permute-start.9) | collective-permute-done | bytes 458784 | tf_op jit(solution)/shard_map/ppermute | solution.py:249
  40.9 2.0 %collective-permute-start.11 = (bf16[4,64,896]{2,1,0:T(8,128)(2,1)S(1)}, bf16[4,64,896]{2,1,0:T(8,128)(2,1)S(1)}, u32[]{:S(2)}, u32[]{:S(2)}) collective-permute-start(bf16[4,64,896]{2,1,0:T(8,128)(2,1)S(1)} %collective-permute-done.9.refs_2_), channel_id=1, source_target_pairs={{0,1},{1,0},{2,3},{3,2},{4,5},{5,4},{6,7},{7,6},{8,9},{9,8},{10,11... | collective-permute-start | bytes 1376264 | tf_op jit(solution)/shard_map/ppermute | solution.py:249
  42.9 0.9 %collective-permute-start.4 = (bf16[320,512]{1,0:T(8,128)(2,1)S(1)}, bf16[320,512]{1,0:T(8,128)(2,1)S(1)}, u32[]{:S(2)}, u32[]{:S(2)}) collective-permute-start(bf16[320,512]{1,0:T(8,128)(2,1)S(1)} %get-tuple-element.35.refs_1_), channel_id=1, source_target_pairs={{0,4},{1,5},{2,6},{3,7},{4,8},{5,9},{6,10},{7,11},{8,12},{9,13},{1... | collective-permute-start | bytes 983048 | tf_op jit(solution)/shard_map/ppermute | solution.py:249
  43.8 0.0 collective-permute-done.3.refs_2_
  43.8 0.8 %collective-permute-start.5 = (bf16[320,512]{1,0:T(8,128)(2,1)S(1)}, bf16[320,512]{1,0:T(8,128)(2,1)S(1)}, u32[]{:S(2)}, u32[]{:S(2)}) collective-permute-start(bf16[320,512]{1,0:T(8,128)(2,1)S(1)} %collective-permute-done.3.refs_2_), channel_id=1, source_target_pairs={{0,4},{1,5},{2,6},{3,7},{4,8},{5,9},{6,10},{7,11},{8,12},{9,13},{1... | collective-permute-start | bytes 983048 | tf_op jit(solution)/shard_map/ppermute | solution.py:249
  44.6 3.1 %collective-permute-done.6.refs_7_ = bf16[320,512]{1,0:T(8,128)(2,1)S(1)} collective-permute-done((bf16[320,512]{1,0:T(8,128)(2,1)S(1)}, bf16[320,512]{1,0:T(8,128)(2,1)S(1)}, u32[]{:S(2)}, u32[]{:S(2)}) %collective-permute-start.6) | collective-permute-done | bytes 327712 | tf_op jit(solution)/shard_map/ppermute | solution.py:249
  47.8 3.4 %collective-permute-start.7 = (bf16[320,512]{1,0:T(8,128)(2,1)S(1)}, bf16[320,512]{1,0:T(8,128)(2,1)S(1)}, u32[]{:S(2)}, u32[]{:S(2)}) collective-permute-start(bf16[320,512]{1,0:T(8,128)(2,1)S(1)} %collective-permute-done.6.refs_7_), channel_id=1, source_target_pairs={{0,12},{1,13},{2,14},{3,15},{4,0},{5,1},{6,2},{7,3},{8,4},{9,5},{1... | collective-permute-start | bytes 983048 | tf_op jit(solution)/shard_map/ppermute | solution.py:249
  51.2 0.9 %collective-permute-done.4.refs_3_ = bf16[320,512]{1,0:T(8,128)(2,1)S(1)} collective-permute-done((bf16[320,512]{1,0:T(8,128)(2,1)S(1)}, bf16[320,512]{1,0:T(8,128)(2,1)S(1)}, u32[]{:S(2)}, u32[]{:S(2)}) %collective-permute-start.4) | collective-permute-done | bytes 327712 | tf_op jit(solution)/shard_map/ppermute | solution.py:249
  52.1 0.0 collective-permute-done.10.refs_3_
  52.1 7.0 %collective-permute-done.5.refs_4_ = bf16[320,512]{1,0:T(8,128)(2,1)S(1)} collective-permute-done((bf16[320,512]{1,0:T(8,128)(2,1)S(1)}, bf16[320,512]{1,0:T(8,128)(2,1)S(1)}, u32[]{:S(2)}, u32[]{:S(2)}) %collective-permute-start.5) | collective-permute-done | bytes 327712 | tf_op jit(solution)/shard_map/ppermute | solution.py:249
  59.1 0.4 shard_map.52.refs_0_
  59.6 2.2 %collective-permute-start.12 = (bf16[2560,512]{1,0:T(8,128)(2,1)S(1)}, bf16[2560,512]{1,0:T(8,128)(2,1)S(1)}, u32[]{:S(2)}, u32[]{:S(2)}) collective-permute-start(bf16[2560,512]{1,0:T(8,128)(2,1)S(1)} %shard_map.52.refs_0_), channel_id=1, source_target_pairs={{0,1},{1,0},{2,3},{3,2},{4,5},{5,4},{6,7},{7,6},{8,9},{9,8},{10,11... | collective-permute-start | bytes 7864328 | tf_op jit(solution)/shard_map/ppermute | solution.py:249
  61.8 3.6 %shard_map.53 = (bf16[8,8,4,48,512]{4,3,2,1,0:T(8,128)(2,1)}, bf16[8,448,512]{2,1,0:T(8,128)(2,1)}) custom-call(bf16[2560,512]{1,0:T(8,128)(2,1)S(1)} %shard_map.52.refs_0_, bf16[4,64,896]{2,1,0:T(8,128)(2,1)S(1)} %get-tuple-element.46.refs_1_, bf16[4,64,896]{2,1,0:T(8,128)(2,1)S(1)} %collective-permute-done.9.refs_2_, ...), custom_call_target="tpu_custom_call" | custom-call | flops 1024 | bytes 1024 | tf_op jit(solution)/shard_map/pallas_call | solution.py:227
  65.4 0.9 %collective-permute-done.12.refs_0_ = bf16[2560,512]{1,0:T(8,128)(2,1)S(1)} collective-permute-done((bf16[2560,512]{1,0:T(8,128)(2,1)S(1)}, bf16[2560,512]{1,0:T(8,128)(2,1)S(1)}, u32[]{:S(2)}, u32[]{:S(2)}) %collective-permute-start.12) | collective-permute-done | bytes 2621472 | tf_op jit(solution)/shard_map/ppermute | solution.py:249
  66.3 3.6 %shard_map.54 = (bf16[8,8,4,48,512]{4,3,2,1,0:T(8,128)(2,1)}, bf16[8,448,512]{2,1,0:T(8,128)(2,1)}) custom-call(bf16[2560,512]{1,0:T(8,128)(2,1)S(1)} %collective-permute-done.12.refs_0_, bf16[4,64,896]{2,1,0:T(8,128)(2,1)S(1)} %get-tuple-element.46.refs_1_, ...), custom_call_target="tpu_custom_call", output_to_operand_aliasing={{0}: (5, {}), {1}: (6, {})} | custom-call | flops 1024 | bytes 1024 | tf_op jit(solution)/shard_map/pallas_call | solution.py:227
  (6 shorter events, 0.0 us)
Async XLA Ops:
  3.2 24.0 %all-to-all-start = ((bf16[32,16,640]{2,1,0:T(8,128)(2,1)}), bf16[32,16,640]{2,1,0:T(8,128)(2,1)S(1)}, u32[]{:S(2)}, u32[]{:S(2)}) async-start(bf16[32,16,640]{2,1,0:T(8,128)(2,1)} %get-tuple-element.28), calls=%async_computation | async-start | bytes 1310720 | tf_op jit(solution)/shard_map/all_to_all | solution.py:253
  12.8 8.5 %collective-permute-start = (bf16[64,1792]{1,0:T(8,128)(2,1)}, bf16[64,1792]{1,0:T(8,128)(2,1)S(1)}, u32[]{:S(2)}, u32[]{:S(2)}) collective-permute-start(bf16[64,1792]{1,0:T(8,128)(2,1)} %get-tuple-element.30), channel_id=1, source_target_pairs={{0,4},{1,5},{2,6},{3,7},{4,8},{5,9},{6,10},{7,11},{8,12},{9,13},{1... | collective-permute-start | bytes 688136 | tf_op jit(solution)/shard_map/ppermute | solution.py:249
  14.1 13.1 %collective-permute-start.1 = (bf16[64,1792]{1,0:T(8,128)(2,1)}, bf16[64,1792]{1,0:T(8,128)(2,1)S(1)}, u32[]{:S(2)}, u32[]{:S(2)}) collective-permute-start(bf16[64,1792]{1,0:T(8,128)(2,1)} %get-tuple-element.31), channel_id=1, source_target_pairs={{0,8},{1,9},{2,10},{3,11},{4,12},{5,13},{6,14},{7,15},{8,0},{9,1},... | collective-permute-start | bytes 688136 | tf_op jit(solution)/shard_map/ppermute | solution.py:249
  16.5 10.6 %collective-permute-start.2 = (bf16[64,1792]{1,0:T(8,128)(2,1)}, bf16[64,1792]{1,0:T(8,128)(2,1)S(1)}, u32[]{:S(2)}, u32[]{:S(2)}) collective-permute-start(bf16[64,1792]{1,0:T(8,128)(2,1)} %get-tuple-element.32), channel_id=1, source_target_pairs={{0,12},{1,13},{2,14},{3,15},{4,0},{5,1},{6,2},{7,3},{8,4},{9,5},{1... | collective-permute-start | bytes 688136 | tf_op jit(solution)/shard_map/ppermute | solution.py:249
  28.4 12.5 %collective-permute-start.9 = (bf16[4,64,896]{2,1,0:T(8,128)(2,1)S(1)}, bf16[4,64,896]{2,1,0:T(8,128)(2,1)S(1)}, u32[]{:S(2)}, u32[]{:S(2)}) collective-permute-start(bf16[4,64,896]{2,1,0:T(8,128)(2,1)S(1)} %get-tuple-element.54), channel_id=1, source_target_pairs={{0,2},{1,3},{2,0},{3,1},{4,6},{5,7},{6,4},{7,5},{8,10},{9,11},{10,... | collective-permute-start | bytes 1376264 | tf_op jit(solution)/shard_map/ppermute | solution.py:249
  31.7 11.2 %collective-permute-start.8 = (bf16[320,512]{1,0:T(8,128)(2,1)S(1)}, bf16[320,512]{1,0:T(8,128)(2,1)S(1)}, u32[]{:S(2)}, u32[]{:S(2)}) collective-permute-start(bf16[320,512]{1,0:T(8,128)(2,1)S(1)} %get-tuple-element.34.refs_0_), channel_id=1, source_target_pairs={{0,12},{1,13},{2,14},{3,15},{4,0},{5,1},{6,2},{7,3},{8,4},{9,5},{1... | collective-permute-start | bytes 983048 | tf_op jit(solution)/shard_map/ppermute | solution.py:249
  34.5 9.4 %collective-permute-start.3 = (bf16[320,512]{1,0:T(8,128)(2,1)S(1)}, bf16[320,512]{1,0:T(8,128)(2,1)S(1)}, u32[]{:S(2)}, u32[]{:S(2)}) collective-permute-start(bf16[320,512]{1,0:T(8,128)(2,1)S(1)} %get-tuple-element.34.refs_0_), channel_id=1, source_target_pairs={{0,4},{1,5},{2,6},{3,7},{4,8},{5,9},{6,10},{7,11},{8,12},{9,13},{1... | collective-permute-start | bytes 983048 | tf_op jit(solution)/shard_map/ppermute | solution.py:249
  34.5 13.3 %collective-permute-start.6 = (bf16[320,512]{1,0:T(8,128)(2,1)S(1)}, bf16[320,512]{1,0:T(8,128)(2,1)S(1)}, u32[]{:S(2)}, u32[]{:S(2)}) collective-permute-start(bf16[320,512]{1,0:T(8,128)(2,1)S(1)} %get-tuple-element.35.refs_1_), channel_id=1, source_target_pairs={{0,12},{1,13},{2,14},{3,15},{4,0},{5,1},{6,2},{7,3},{8,4},{9,5},{1... | collective-permute-start | bytes 983048 | tf_op jit(solution)/shard_map/ppermute | solution.py:249
  37.1 14.9 %collective-permute-start.10 = (bf16[4,64,896]{2,1,0:T(8,128)(2,1)S(1)}, bf16[4,64,896]{2,1,0:T(8,128)(2,1)S(1)}, u32[]{:S(2)}, u32[]{:S(2)}) collective-permute-start(bf16[4,64,896]{2,1,0:T(8,128)(2,1)S(1)} %get-tuple-element.46.refs_1_), channel_id=1, source_target_pairs={{0,1},{1,0},{2,3},{3,2},{4,5},{5,4},{6,7},{7,6},{8,9},{9,8},{10,11... | collective-permute-start | bytes 1376264 | tf_op jit(solution)/shard_map/ppermute | solution.py:249
  40.9 18.2 %collective-permute-start.11 = (bf16[4,64,896]{2,1,0:T(8,128)(2,1)S(1)}, bf16[4,64,896]{2,1,0:T(8,128)(2,1)S(1)}, u32[]{:S(2)}, u32[]{:S(2)}) collective-permute-start(bf16[4,64,896]{2,1,0:T(8,128)(2,1)S(1)} %collective-permute-done.9.refs_2_), channel_id=1, source_target_pairs={{0,1},{1,0},{2,3},{3,2},{4,5},{5,4},{6,7},{7,6},{8,9},{9,8},{10,11... | collective-permute-start | bytes 1376264 | tf_op jit(solution)/shard_map/ppermute | solution.py:249
  42.9 9.2 %collective-permute-start.4 = (bf16[320,512]{1,0:T(8,128)(2,1)S(1)}, bf16[320,512]{1,0:T(8,128)(2,1)S(1)}, u32[]{:S(2)}, u32[]{:S(2)}) collective-permute-start(bf16[320,512]{1,0:T(8,128)(2,1)S(1)} %get-tuple-element.35.refs_1_), channel_id=1, source_target_pairs={{0,4},{1,5},{2,6},{3,7},{4,8},{5,9},{6,10},{7,11},{8,12},{9,13},{1... | collective-permute-start | bytes 983048 | tf_op jit(solution)/shard_map/ppermute | solution.py:249
  43.8 15.3 %collective-permute-start.5 = (bf16[320,512]{1,0:T(8,128)(2,1)S(1)}, bf16[320,512]{1,0:T(8,128)(2,1)S(1)}, u32[]{:S(2)}, u32[]{:S(2)}) collective-permute-start(bf16[320,512]{1,0:T(8,128)(2,1)S(1)} %collective-permute-done.3.refs_2_), channel_id=1, source_target_pairs={{0,4},{1,5},{2,6},{3,7},{4,8},{5,9},{6,10},{7,11},{8,12},{9,13},{1... | collective-permute-start | bytes 983048 | tf_op jit(solution)/shard_map/ppermute | solution.py:249
  47.8 11.3 %collective-permute-start.7 = (bf16[320,512]{1,0:T(8,128)(2,1)S(1)}, bf16[320,512]{1,0:T(8,128)(2,1)S(1)}, u32[]{:S(2)}, u32[]{:S(2)}) collective-permute-start(bf16[320,512]{1,0:T(8,128)(2,1)S(1)} %collective-permute-done.6.refs_7_), channel_id=1, source_target_pairs={{0,12},{1,13},{2,14},{3,15},{4,0},{5,1},{6,2},{7,3},{8,4},{9,5},{1... | collective-permute-start | bytes 983048 | tf_op jit(solution)/shard_map/ppermute | solution.py:249
  59.6 6.8 %collective-permute-start.12 = (bf16[2560,512]{1,0:T(8,128)(2,1)S(1)}, bf16[2560,512]{1,0:T(8,128)(2,1)S(1)}, u32[]{:S(2)}, u32[]{:S(2)}) collective-permute-start(bf16[2560,512]{1,0:T(8,128)(2,1)S(1)} %shard_map.52.refs_0_), channel_id=1, source_target_pairs={{0,1},{1,0},{2,3},{3,2},{4,5},{5,4},{6,7},{7,6},{8,9},{9,8},{10,11... | collective-permute-start | bytes 7864328 | tf_op jit(solution)/shard_map/ppermute | solution.py:249

commit v4 on v3

v4 whole, which is shorter than its diff:
```python
import jax
import jax.numpy as jnp
from jax import lax
from jax.experimental import pallas as pl
from jax.experimental.pallas import tpu as pltpu
from jax.sharding import Mesh, PartitionSpec as P

QL = 1536
KVL = 512
NOPE = 128
VD = 128
X, ZH, ZL, Y, C = 4, 2, 2, 4, 2
BULK = ("x", "zh", "c")
OWNERS = ("zl", "y", "zh", "c")
F = ZL * Y
HEADS = 8
HALF = 4
WIDE = HALF * NOPE
Q_ROWS, KV_ROWS = 12, 4
Q_BLOCK = ZH * C * Q_ROWS
Q_ALL = F * Q_BLOCK
L_BLOCK = ZH * C * KV_ROWS
ROWS = Q_ALL + 2 * F * L_BLOCK
D_PART = 448
bf16 = jnp.bfloat16
PACK_MIB = 56
EXTRA = 48
VMEM = pl.BlockSpec(memory_space=pltpu.VMEM)
ANY = pl.BlockSpec(memory_space=pl.ANY)


def shifts(dx, dz, dc):
    at = lambda x, z, c: (x * ZH + z) * C + c
    return [
        (at(x, z, c), at((x + dx) % X, (z + dz) % ZH, (c + dc) % C))
        for x in range(X)
        for z in range(ZH)
        for c in range(C)
    ]


COST = pl.CostEstimate(flops=1024, bytes_accessed=1024, transcendentals=0)


def limit(mib):
    return pltpu.CompilerParams(vmem_limit_bytes=mib * 2**20)


def pack_kernel(q_hbm, kv_hbm, o_hbm, out_ref, *refs):
    o_refs, (q_ref, kv_ref, sems) = refs[:X], refs[X:]
    kv_copy = pltpu.make_async_copy(kv_hbm, kv_ref, sems.at[0])
    q_copy = pltpu.make_async_copy(q_hbm, q_ref, sems.at[1])
    kv_copy.start()
    q_copy.start()
    copies = []
    o_cols = o_hbm.shape[1] // X
    for d in range(X):
        at = pl.multiple_of(lax.rem(lax.axis_index("x") + d, X) * o_cols, 128)
        copies.append(
            pltpu.make_async_copy(o_hbm.at[:, pl.ds(at, o_cols)], o_refs[d], sems.at[2 + d])
        )
        copies[d].start()
    kv_copy.wait()
    for n in range(F * C):
        for z in range(ZH):
            at = (n // C * ZH + z) * C + n % C
            out_ref[at, Q_ROWS:, :WIDE] = kv_ref[:, n * 1024 : n * 1024 + WIDE]
            for j in range(4):
                lane = n * 1024 + WIDE + j * 128
                out_ref[at, j * 4 : (j + 1) * 4, WIDE:] = kv_ref[:, lane : lane + 128]
    q_copy.wait()
    for n in range(F * C):
        for z in range(ZH):
            at = (n // C * ZH + z) * C + n % C
            out_ref[at, :Q_ROWS, :WIDE] = q_ref[:, n * WIDE : (n + 1) * WIDE]
    for copy in copies:
        copy.wait()


def pack(q, kv, o):
    o_cols = o.shape[1] // X
    out = pl.pallas_call(
        pack_kernel,
        in_specs=[ANY] * 3,
        out_specs=[VMEM] * (X + 1),
        out_shape=[jax.ShapeDtypeStruct((F * ZH * C, 16, 640), bf16)]
        + [jax.ShapeDtypeStruct((o.shape[0], o_cols), bf16)] * X,
        scratch_shapes=[
            pltpu.VMEM(q.shape, bf16),
            pltpu.VMEM(kv.shape, bf16),
            pltpu.SemaphoreType.DMA((2 + X,)),
        ],
        compiler_params=limit(PACK_MIB),
        cost_estimate=COST,
    )(q, kv, o)
    return out[0], out[1:]


def unpack_kernel(packed_ref, left_ref, right_ref, half_left_ref, half_right_ref, out, half_out):
    half_out[ROWS // 2 :] = jnp.zeros((EXTRA, WIDE), bf16)
    for g in range(2):
        packed = packed_ref[g * 256 : (g + 1) * 256]
        for left_by, right_by, ref in (
            (left_ref, right_ref, out),
            (half_left_ref, half_right_ref, half_out),
        ):
            left = jnp.dot(left_by[...], packed[:, :WIDE], preferred_element_type=jnp.float32)
            right = jnp.dot(right_by[...], packed[:, WIDE:], preferred_element_type=jnp.float32)
            left, right = left.astype(bf16), right.astype(bf16)
            rows_l = left_by.shape[0] // 4
            rows_q = 3 * rows_l
            ref[g * rows_q : (g + 1) * rows_q] = left[:rows_q]
            at = (2 * 3 + g) * rows_l
            ref[at : at + rows_l] = left[rows_q:]
            at += 2 * rows_l
            for j in range(4):
                lanes = slice(j * 128, (j + 1) * 128)
                ref[at : at + rows_l, lanes] = right[j * rows_l : (j + 1) * rows_l]


def unpack(packed, zh):
    column = jnp.arange(256)[None, :]

    def select(sources, first):
        size = sources * 16
        row = jnp.arange(4 * size)
        block = lambda n: n // sources * 4 + n % sources + first
        of_q = block(row // Q_ROWS) * 16 + row % Q_ROWS
        r = row % size
        of_kv = block(r // KV_ROWS) * 16 + r % KV_ROWS
        left = jnp.where(row < 3 * size, of_q, of_kv + Q_ROWS)
        right = of_kv + row // size * 4
        return [(source[:, None] == column).astype(bf16) for source in (left, right)]

    return pl.pallas_call(
        unpack_kernel,
        out_shape=[
            jax.ShapeDtypeStruct((ROWS, WIDE), bf16),
            jax.ShapeDtypeStruct((ROWS // 2 + EXTRA, WIDE), bf16),
        ],
        compiler_params=limit(8),
        cost_estimate=COST,
    )(packed, *select(4, 0), *select(2, zh * 2))


def sort_kernel(own, right, left, same_ref, cross_ref, by_q_ref, by_l_ref, out, far, kv):
    half_q, half_l = Q_ALL // 4, F * L_BLOCK // 2
    for g in range(2):
        at = slice(g * half_q, (g + 1) * half_q)
        block = jnp.concatenate([same_ref[at], cross_ref[at]], axis=0)
        block = jnp.dot(by_q_ref[...], block, preferred_element_type=jnp.float32)
        far[2 * g * half_q : 2 * (g + 1) * half_q] = block.astype(bf16)
    for h in range(2):
        at = slice(Q_ALL // 2 + h * half_l, Q_ALL // 2 + (h + 1) * half_l)
        block = jnp.concatenate([same_ref[at], cross_ref[at]], axis=0)
        block = jnp.dot(by_l_ref[...], block, preferred_element_type=jnp.float32)
        at = Q_ALL + 2 * h * half_l
        far[at : at + 2 * half_l] = block.astype(bf16)
    for d, ref in enumerate((own, right, far, left)):
        xs = lax.rem(lax.axis_index("x") - d + X, X)
        for f in range(F):
            at = pl.multiple_of(f * (X * L_BLOCK) + xs * L_BLOCK, L_BLOCK)
            for h in range(2):
                source = Q_ALL + (h * F + f) * L_BLOCK
                rows = ref[source : source + L_BLOCK]
                kv[pl.ds(at, L_BLOCK), h * WIDE : (h + 1) * WIDE] = rows
        out[2 * KVL + d * Q_ALL : 2 * KVL + (d + 1) * Q_ALL] = ref[:Q_ALL]
    for k in range(HALF):
        out[k * NOPE : (k + 1) * NOPE] = kv[:, k * 256 : k * 256 + NOPE].T
        out[KVL : 2 * KVL, k * VD : (k + 1) * VD] = kv[:, k * 256 + NOPE : (k + 1) * 256]


def interleave(blocks, size, zh):
    row = jnp.arange(2 * blocks * size)
    z = row // size % ZH
    source = jnp.where(z == zh, 0, blocks * size) + row // (ZH * size) * size + row % size
    return (source[:, None] == row[None, :]).astype(bf16)


def sort_rows(zh, own, right, left, same, cross):
    return pl.pallas_call(
        sort_kernel,
        out_shape=jax.ShapeDtypeStruct((2 * KVL + X * Q_ALL, WIDE), bf16),
        scratch_shapes=[pltpu.VMEM((ROWS, WIDE), bf16), pltpu.VMEM((KVL, 1024), bf16)],
        compiler_params=limit(12),
        cost_estimate=COST,
    )(own, right, left, same, cross, interleave(F // 2, 24, zh), interleave(F, 8, zh))


def sender(sems):
    copies = []

    def send(source, target):
        copy = pltpu.make_async_copy(source, target, sems.at[len(copies)])
        copy.start()
        copies.append(copy)

    return copies, send


def query_blocks(x, half, rows_ref, q_out, blocks, send):
    for d in range(X):
        xs = lax.rem(x - d + X, X)
        first = 2 * KVL + d * Q_ALL
        for k in range(HALF):
            lanes = slice(k * NOPE, (k + 1) * NOPE)
            block = jnp.dot(
                rows_ref[first : first + Q_ALL, lanes],
                rows_ref[lanes],
                preferred_element_type=jnp.float32,
            )
            at = d * HALF + k
            blocks[at] = block.astype(bf16).reshape(F, Q_BLOCK, KVL)
            send(blocks.at[at], q_out.at[half * HALF + k, :, xs])


def query_kernel(rows_ref, q_out, blocks, sems):
    copies, send = sender(sems)
    query_blocks(lax.axis_index("x"), lax.axis_index("c"), rows_ref, q_out, blocks, send)
    for copy in copies:
        copy.wait()


def query(rows):
    return pl.pallas_call(
        query_kernel,
        in_specs=[VMEM],
        out_specs=ANY,
        scratch_shapes=[
            pltpu.VMEM((X * HALF, F, Q_BLOCK, KVL), bf16),
            pltpu.SemaphoreType.DMA((X * HALF,)),
        ],
        out_shape=jax.ShapeDtypeStruct((HEADS, F, X, Q_BLOCK, KVL), bf16),
        compiler_params=limit(16),
        cost_estimate=COST,
    )(rows)


def rest_kernel(own_ref, other_ref, o_own_ref, o_other_ref, _, q_out, d_out, *scratch):
    blocks, heads, wide, sems = scratch
    x, zh, c = (lax.axis_index(a) for a in BULK)
    copies, send = sender(sems)
    lanes = pl.ds(pl.multiple_of(c * 384, 128), 512)
    own_at = pl.ds(pl.multiple_of(c * 64, 64), 64)
    other_at = pl.ds(pl.multiple_of((1 - c) * 64, 64), 64)
    part = pl.ds(pl.multiple_of(c * 64, 64), D_PART)
    query_blocks(x, 1 - c, other_ref, q_out, blocks, send)
    for n, (rows_ref, half) in enumerate(((own_ref, c), (other_ref, 1 - c))):
        for k in range(HALF):
            d = lax.rem(x - (2 * half + k // 2) + X, X)
            z = lax.rem(zh + k, 2)
            at = n * HALF + k
            heads[at, own_at, :] = o_own_ref[z, d, :, lanes]
            heads[at, other_at, :] = o_other_ref[z, d, :, lanes]
        for k in range(HALF):
            at = n * HALF + k
            value = rows_ref[KVL : 2 * KVL, k * VD : (k + 1) * VD]
            wide[at] = lax.dot_general(
                heads[at], value, (((0,), (1,)), ((), ())), preferred_element_type=jnp.float32
            ).astype(bf16)
            send(wide.at[at, part], d_out.at[half * HALF + k])
    for copy in copies:
        copy.wait()


def rest(rows, rows_other, o_own, o_other, q_out):
    return pl.pallas_call(
        rest_kernel,
        in_specs=[VMEM] * 4 + [ANY],
        out_specs=[ANY, ANY],
        scratch_shapes=[
            pltpu.VMEM((X * HALF, F, Q_BLOCK, KVL), bf16),
            pltpu.VMEM((HEADS, VD, 512), bf16),
            pltpu.VMEM((HEADS, 512, KVL), bf16),
            pltpu.SemaphoreType.DMA((X * HALF + HEADS,)),
        ],
        out_shape=[
            jax.ShapeDtypeStruct((HEADS, F, X, Q_BLOCK, KVL), bf16),
            jax.ShapeDtypeStruct((HEADS, D_PART, KVL), bf16),
        ],
        input_output_aliases={4: 0},
        compiler_params=limit(20),
        cost_estimate=COST,
    )(rows, rows_other, o_own, o_other, q_out)


def on_device(q_nope, kv_up, o_proj):
    zh = lax.axis_index("zh")
    over = lambda a, *d: lax.ppermute(a, BULK, shifts(*d))
    core = (0, 0, 1)

    packed, o_send = pack(q_nope, kv_up, o_proj)
    packed = lax.all_to_all(packed, OWNERS, split_axis=0, concat_axis=0, tiled=True)
    o_x = [o_send[0]] + [over(o_send[d], d, 0, 0) for d in (1, 2, 3)]
    packed, o_x = lax.optimization_barrier((packed, o_x))

    own, part = unpack(packed.reshape(F * ZH * C * 16, 640), zh)
    same = over(part, 2, 0, 0)
    near = [over(own, 1, 0, 0), over(own, 3, 0, 0)]
    cross = over(same, 0, 1, 0)
    half = lambda z: jnp.stack(
        [lax.dynamic_slice_in_dim(o, z * (2 * D_PART), 2 * D_PART, 1) for o in o_x]
    )
    o_z = over(half(1 - zh), 0, 1, 0)
    near, same, cross, o_z = lax.optimization_barrier((near, same, cross, o_z))

    o_own = jnp.stack([half(zh), o_z])
    o_other = over(o_own, *core)
    rows = sort_rows(zh, own, *near, same, cross)
    rows_other = over(rows, *core)
    q_out = query(rows)
    q_out, d_out = rest(rows, rows_other, o_own, o_other, q_out)
    return q_out.reshape(HEADS, QL, KVL), d_out.transpose(0, 2, 1)


def solution(mesh):
    fine = Mesh(mesh.devices.reshape(ZL, Y, X, ZH, C), ("zl", "y", "x", "zh", "c"))
    rows = P(("zl", "y", "x", "zh", "c"), None)
    return jax.shard_map(
        on_device,
        mesh=fine,
        in_specs=(rows, rows, rows),
        out_specs=(P(("zl", "y"), None, None), P(("zl", "y"), None, BULK)),
        check_vma=False,
    )
```

time: 70.2 us -> 66.1 us (0.942)
  starting transfers between devices: 33.7 us -> 24.8 us
  waiting for transfers between devices: 23.6 us -> 27.4 us
  local copies, waits for them, and re-layouts: 0.13 us -> 1.05 us
    ppermute x13 -> x10, starting transfers between devices: 24.1 us -> 15.2 us  [on_device(): over = lambda a, *d: lax.ppermute(a, BULK, shifts(*d))]
    ppermute x13 -> x10, waiting for transfers between devices: 23.6 us -> 27.4 us  [on_device(): over = lambda a, *d: lax.ppermute(a, BULK, shifts(*d))]
    another operation x0 -> x2, local copies, waits for them, and re-layouts: none -> 1.05 us  [on_device(): jnp.stack([lax.dynamic_slice_in_dim(o, z * (2 * D_PART), 2 * D_PART, 1) f...]
    another operation x1 -> x3, other arithmetic: 1.06 us -> 0.24 us  [the longest x2 0.17 us: on_device(): o_own = jnp.stack([half(zh), o_z])]
  transfers between devices with their start and end apart: 14 -> 11, of which waited for: 7 -> 7; matrix products, arithmetic and copies ran while one was open for 0% -> 3% of each run, Pallas kernels for 6% -> 5%
where the time goes in v4:
time: 66.1 us; the launch traced here: 65.8 us
  waiting for transfers between devices  27.4 us (41%)
  starting transfers between devices  24.8 us (38%)
  Pallas kernels  10.9 us (16%)
  local copies, waits for them, and re-layouts  1.05 us (2%)
  other arithmetic  0.85 us (1%)
  between operations  0.77 us (1%)
    ppermute x10, waiting for transfers between devices, on_device(): over = lambda a, *d: lax.ppermute(a, BULK, shifts(*d))  27.4 us
    ppermute x10, starting transfers between devices, on_device(): over = lambda a, *d: lax.ppermute(a, BULK, shifts(*d))  15.2 us
    all_to_all x1, starting transfers between devices, on_device(): lax.all_to_all(packed, OWNERS, split_axis=0, concat_axis=0, tiled=True)  9.61 us
    pallas_call x1, Pallas kernels, rest(): pl.pallas_call(rest_kernel, in_specs=[VMEM] * 4 + [ANY], out_specs=[ANY,...  4.2 us
    pallas_call x1, Pallas kernels, query(): pl.pallas_call(query_kernel, in_specs=[VMEM], out_specs=ANY, scratch_shap...  3.02 us
    pallas_call x1, Pallas kernels, pack(): pl.pallas_call(pack_kernel, in_specs=[ANY] * 3, out_specs=[VMEM] * (X + 1...  2.52 us
  transfers between devices with their start and end apart: 11, of which 7 were waited for; matrix products, arithmetic and copies ran while one was open for 3% of the time, Pallas kernels for 5%

profile of v4, /device:TPU:1, one launch (start us, length us, event | category | flops | bytes accessed | tf_op | source)
XLA Modules:
  0.0 65.8 jit_solution(3356759155680665671)
XLA Ops:
  0.6 2.5 %shard_map.50 = (bf16[32,16,640]{2,1,0:T(8,128)(2,1)}, bf16[64,1792]{1,0:T(8,128)(2,1)}, bf16[64,1792]{1,0:T(8,128)(2,1)}, bf16[64,1792]{1,0:T(8,128)(2,1)}, bf16[64,1792]{1,0:T(8,128)(2,1)}) custom-call(bf16[12,8192]{1,0:T(8,128)(2,1)} %q_hbm.1, bf16[4,16384]{1,0:T(4,128)(2,1)} %kv_hbm.1, bf16[64,7168]{1,0:T(8,128)(2,1)} %o_hbm.1), custom_call_target="tpu_custom_call" | custom-call | flops 1024 | bytes 1024 | tf_op jit(solution)/shard_map/pallas_call | solution.py:82
  3.2 9.6 %all-to-all-start = ((bf16[32,16,640]{2,1,0:T(8,128)(2,1)}), bf16[32,16,640]{2,1,0:T(8,128)(2,1)S(1)}, u32[]{:S(2)}, u32[]{:S(2)}) async-start(bf16[32,16,640]{2,1,0:T(8,128)(2,1)} %get-tuple-element.21), calls=%async_computation | async-start | bytes 1310720 | tf_op jit(solution)/shard_map/all_to_all | solution.py:293
  12.8 1.3 %collective-permute-start = (bf16[64,1792]{1,0:T(8,128)(2,1)}, bf16[64,1792]{1,0:T(8,128)(2,1)S(1)}, u32[]{:S(2)}, u32[]{:S(2)}) collective-permute-start(bf16[64,1792]{1,0:T(8,128)(2,1)} %get-tuple-element.23), channel_id=1, source_target_pairs={{0,4},{1,5},{2,6},{3,7},{4,8},{5,9},{6,10},{7,11},{8,12},{9,13},{1... | collective-permute-start | bytes 688136 | tf_op jit(solution)/shard_map/ppermute | solution.py:289
  14.1 2.5 %collective-permute-start.1 = (bf16[64,1792]{1,0:T(8,128)(2,1)}, bf16[64,1792]{1,0:T(8,128)(2,1)S(1)}, u32[]{:S(2)}, u32[]{:S(2)}) collective-permute-start(bf16[64,1792]{1,0:T(8,128)(2,1)} %get-tuple-element.24), channel_id=1, source_target_pairs={{0,8},{1,9},{2,10},{3,11},{4,12},{5,13},{6,14},{7,15},{8,0},{9,1},... | collective-permute-start | bytes 688136 | tf_op jit(solution)/shard_map/ppermute | solution.py:289
  16.5 1.2 %collective-permute-start.2 = (bf16[64,1792]{1,0:T(8,128)(2,1)}, bf16[64,1792]{1,0:T(8,128)(2,1)S(1)}, u32[]{:S(2)}, u32[]{:S(2)}) collective-permute-start(bf16[64,1792]{1,0:T(8,128)(2,1)} %get-tuple-element.25), channel_id=1, source_target_pairs={{0,12},{1,13},{2,14},{3,15},{4,0},{5,1},{6,2},{7,3},{8,4},{9,5},{1... | collective-permute-start | bytes 688136 | tf_op jit(solution)/shard_map/ppermute | solution.py:289
  17.7 0.1 fusion.left_ref
  17.8 0.1 fusion.3.half_left_ref
  17.9 0.1 fusion.4.half_right_ref
  18.0 0.1 fusion.1.right_ref
  18.1 3.1 %collective-permute-done = bf16[64,1792]{1,0:T(8,128)(2,1)S(1)} collective-permute-done((bf16[64,1792]{1,0:T(8,128)(2,1)}, bf16[64,1792]{1,0:T(8,128)(2,1)S(1)}, u32[]{:S(2)}, u32[]{:S(2)}) %collective-permute-start) | collective-permute-done | bytes 229408 | tf_op jit(solution)/shard_map/ppermute | solution.py:289
  21.2 5.9 %collective-permute-done.1 = bf16[64,1792]{1,0:T(8,128)(2,1)S(1)} collective-permute-done((bf16[64,1792]{1,0:T(8,128)(2,1)}, bf16[64,1792]{1,0:T(8,128)(2,1)S(1)}, u32[]{:S(2)}, u32[]{:S(2)}) %collective-permute-start.1) | collective-permute-done | bytes 229408 | tf_op jit(solution)/shard_map/ppermute | solution.py:289
  27.1 0.5 shard_map.51
  27.6 2.2 %collective-permute-start.5 = (bf16[368,512]{1,0:T(8,128)(2,1)S(1)}, bf16[368,512]{1,0:T(8,128)(2,1)S(1)}, u32[]{:S(2)}, u32[]{:S(2)}) collective-permute-start(bf16[368,512]{1,0:T(8,128)(2,1)S(1)} %get-tuple-element.28), channel_id=1, source_target_pairs={{0,8},{1,9},{2,10},{3,11},{4,12},{5,13},{6,14},{7,15},{8,0},{9,1},... | collective-permute-start | bytes 1130504 | tf_op jit(solution)/shard_map/ppermute | solution.py:289
  29.8 1.2 %collective-permute-start.4 = (bf16[640,512]{1,0:T(8,128)(2,1)S(1)}, bf16[640,512]{1,0:T(8,128)(2,1)S(1)}, u32[]{:S(2)}, u32[]{:S(2)}) collective-permute-start(bf16[640,512]{1,0:T(8,128)(2,1)S(1)} %get-tuple-element.27.own), channel_id=1, source_target_pairs={{0,12},{1,13},{2,14},{3,15},{4,0},{5,1},{6,2},{7,3},{8,4},{9,5},{1... | collective-permute-start | bytes 1966088 | tf_op jit(solution)/shard_map/ppermute | solution.py:289
  31.0 0.2 collective-permute-start.3
  31.2 1.0 %dynamic-slice_bitcast_fusion.2 = (bf16[1,64,896]{2,1,0:T(8,128)(2,1)S(1)}, bf16[1,64,896]{2,1,0:T(8,128)(2,1)S(1)}, bf16[1,64,896]{2,1,0:T(8,128)(2,1)S(1)}, bf16[1,64,896]{2,1,0:T(8,128)(2,1)S(1)}) fusion(bf16[64,1792]{1,0:T(8,128)(2,1)S(1)} %collective-permute-done, s32[]{:T(128)S(6)} %select_n.340, s32[]{:T(128)S(6)} %select_n.329, ...), kind=kLoop, calls=%fused_computation.15 | loop fusion | bytes 917512 | tf_op jit(solution)/shard_map/stack | solution.py:301
  32.3 0.1 pad_maximum_fusion.1
  32.4 2.9 %collective-permute-start.7 = (bf16[4,64,896]{2,1,0:T(8,128)(2,1)S(1)}, bf16[4,64,896]{2,1,0:T(8,128)(2,1)S(1)}, u32[]{:S(2)}, u32[]{:S(2)}) collective-permute-start(bf16[4,64,896]{2,1,0:T(8,128)(2,1)S(1)} %pad_maximum_fusion.1), channel_id=1, source_target_pairs={{0,2},{1,3},{2,0},{3,1},{4,6},{5,7},{6,4},{7,5},{8,10},{9,11},{10,... | collective-permute-start | bytes 1376264 | tf_op jit(solution)/shard_map/ppermute | solution.py:289
  35.2 3.2 %collective-permute-done.5.same_ref = bf16[368,512]{1,0:T(8,128)(2,1)S(1)} collective-permute-done((bf16[368,512]{1,0:T(8,128)(2,1)S(1)}, bf16[368,512]{1,0:T(8,128)(2,1)S(1)}, u32[]{:S(2)}, u32[]{:S(2)}) %collective-permute-start.5) | collective-permute-done | bytes 376864 | tf_op jit(solution)/shard_map/ppermute | solution.py:289
  38.5 2.6 %collective-permute-start.6 = (bf16[368,512]{1,0:T(8,128)(2,1)S(1)}, bf16[368,512]{1,0:T(8,128)(2,1)S(1)}, u32[]{:S(2)}, u32[]{:S(2)}) collective-permute-start(bf16[368,512]{1,0:T(8,128)(2,1)S(1)} %collective-permute-done.5.same_ref), channel_id=1, source_target_pairs={{0,2},{1,3},{2,0},{3,1},{4,6},{5,7},{6,4},{7,5},{8,10},{9,11},{10,... | collective-permute-start | bytes 1130504 | tf_op jit(solution)/shard_map/ppermute | solution.py:289
  41.1 0.1 fusion.5.by_l_ref
  41.2 0.1 fusion.2.by_q_ref
  41.3 2.5 %collective-permute-done.7 = bf16[4,64,896]{2,1,0:T(8,128)(2,1)S(1)} collective-permute-done((bf16[4,64,896]{2,1,0:T(8,128)(2,1)S(1)}, bf16[4,64,896]{2,1,0:T(8,128)(2,1)S(1)}, u32[]{:S(2)}, u32[]{:S(2)}) %collective-permute-start.7) | collective-permute-done | bytes 458784 | tf_op jit(solution)/shard_map/ppermute | solution.py:289
  43.8 9.5 %collective-permute-done.4.left = bf16[640,512]{1,0:T(8,128)(2,1)S(1)} collective-permute-done((bf16[640,512]{1,0:T(8,128)(2,1)S(1)}, bf16[640,512]{1,0:T(8,128)(2,1)S(1)}, u32[]{:S(2)}, u32[]{:S(2)}) %collective-permute-start.4) | collective-permute-done | bytes 655392 | tf_op jit(solution)/shard_map/ppermute | solution.py:289
  53.3 0.7 collective-permute-done.3.right
  53.9 0.7 %shard_map.52.rows_ref.own_ref = bf16[2560,512]{1,0:T(8,128)(2,1)S(1)} custom-call(bf16[640,512]{1,0:T(8,128)(2,1)S(1)} %get-tuple-element.27.own, bf16[640,512]{1,0:T(8,128)(2,1)S(1)} %collective-permute-done.3.right, bf16[640,512]{1,0:T(8,128)(2,1)S(1)} %collective-permute-done.4.left, bf16[368,512]{1,0:T(8,128)(2,1)S(1)} %collective-permute-done.5.same_ref, ...), custom_call_target="tpu_custom_call" | custom-call | flops 1024 | bytes 1024 | tf_op jit(solution)/shard_map/pallas_call | solution.py:181
  54.7 1.1 %collective-permute-start.8 = (bf16[2560,512]{1,0:T(8,128)(2,1)S(1)}, bf16[2560,512]{1,0:T(8,128)(2,1)S(1)}, u32[]{:S(2)}, u32[]{:S(2)}) collective-permute-start(bf16[2560,512]{1,0:T(8,128)(2,1)S(1)} %shard_map.52.rows_ref.own_ref), channel_id=1, source_target_pairs={{0,1},{1,0},{2,3},{3,2},{4,5},{5,4},{6,7},{7,6},{8,9},{9,8},{10,11... | collective-permute-start | bytes 7864328 | tf_op jit(solution)/shard_map/ppermute | solution.py:289
  55.9 0.1 pad_maximum_fusion.o_own_ref
  56.0 0.1 collective-permute-start.9
  56.1 3.0 %shard_map.53._ = bf16[8,8,4,48,512]{4,3,2,1,0:T(8,128)(2,1)} custom-call(bf16[2560,512]{1,0:T(8,128)(2,1)S(1)} %shard_map.52.rows_ref.own_ref), custom_call_target="tpu_custom_call" | custom-call | flops 1024 | bytes 1024 | tf_op jit(solution)/shard_map/pallas_call | solution.py:225
  59.1 2.5 %collective-permute-done.9.o_other_ref = bf16[2,4,64,896]{3,2,1,0:T(8,128)(2,1)S(1)} collective-permute-done((bf16[2,4,64,896]{3,2,1,0:T(8,128)(2,1)S(1)}, bf16[2,4,64,896]{3,2,1,0:T(8,128)(2,1)S(1)}, u32[]{:S(2)}, u32[]{:S(2)}) %collective-permute-start.9) | collective-permute-done | bytes 917536 | tf_op jit(solution)/shard_map/ppermute | solution.py:289
  61.6 4.2 %shard_map.54 = (bf16[8,8,4,48,512]{4,3,2,1,0:T(8,128)(2,1)}, bf16[8,448,512]{2,1,0:T(8,128)(2,1)}) custom-call(bf16[2560,512]{1,0:T(8,128)(2,1)S(1)} %shard_map.52.rows_ref.own_ref, bf16[2560,512]{1,0:T(8,128)(2,1)S(1)} %collective-permute-done.8.other_ref, bf16[2,4,64,896]{3,2,1,0:T(8,128)(2,1)S(1)} %pad_maximum_fusion.o_own_ref, ...), custom_call_target="tpu_custom_call", output_to_operand_aliasing={{0}: (4, {})} | custom-call | flops 1024 | bytes 1024 | tf_op jit(solution)/shard_map/pallas_call | solution.py:267
  (10 shorter events, 0.2 us)
Async XLA Ops:
  3.2 24.0 %all-to-all-start = ((bf16[32,16,640]{2,1,0:T(8,128)(2,1)}), bf16[32,16,640]{2,1,0:T(8,128)(2,1)S(1)}, u32[]{:S(2)}, u32[]{:S(2)}) async-start(bf16[32,16,640]{2,1,0:T(8,128)(2,1)} %get-tuple-element.21), calls=%async_computation | async-start | bytes 1310720 | tf_op jit(solution)/shard_map/all_to_all | solution.py:293
  12.8 8.5 %collective-permute-start = (bf16[64,1792]{1,0:T(8,128)(2,1)}, bf16[64,1792]{1,0:T(8,128)(2,1)S(1)}, u32[]{:S(2)}, u32[]{:S(2)}) collective-permute-start(bf16[64,1792]{1,0:T(8,128)(2,1)} %get-tuple-element.23), channel_id=1, source_target_pairs={{0,4},{1,5},{2,6},{3,7},{4,8},{5,9},{6,10},{7,11},{8,12},{9,13},{1... | collective-permute-start | bytes 688136 | tf_op jit(solution)/shard_map/ppermute | solution.py:289
  14.1 13.1 %collective-permute-start.1 = (bf16[64,1792]{1,0:T(8,128)(2,1)}, bf16[64,1792]{1,0:T(8,128)(2,1)S(1)}, u32[]{:S(2)}, u32[]{:S(2)}) collective-permute-start(bf16[64,1792]{1,0:T(8,128)(2,1)} %get-tuple-element.24), channel_id=1, source_target_pairs={{0,8},{1,9},{2,10},{3,11},{4,12},{5,13},{6,14},{7,15},{8,0},{9,1},... | collective-permute-start | bytes 688136 | tf_op jit(solution)/shard_map/ppermute | solution.py:289
  16.5 10.6 %collective-permute-start.2 = (bf16[64,1792]{1,0:T(8,128)(2,1)}, bf16[64,1792]{1,0:T(8,128)(2,1)S(1)}, u32[]{:S(2)}, u32[]{:S(2)}) collective-permute-start(bf16[64,1792]{1,0:T(8,128)(2,1)} %get-tuple-element.25), channel_id=1, source_target_pairs={{0,12},{1,13},{2,14},{3,15},{4,0},{5,1},{6,2},{7,3},{8,4},{9,5},{1... | collective-permute-start | bytes 688136 | tf_op jit(solution)/shard_map/ppermute | solution.py:289
  27.6 10.8 %collective-permute-start.5 = (bf16[368,512]{1,0:T(8,128)(2,1)S(1)}, bf16[368,512]{1,0:T(8,128)(2,1)S(1)}, u32[]{:S(2)}, u32[]{:S(2)}) collective-permute-start(bf16[368,512]{1,0:T(8,128)(2,1)S(1)} %get-tuple-element.28), channel_id=1, source_target_pairs={{0,8},{1,9},{2,10},{3,11},{4,12},{5,13},{6,14},{7,15},{8,0},{9,1},... | collective-permute-start | bytes 1130504 | tf_op jit(solution)/shard_map/ppermute | solution.py:289
  29.8 23.5 %collective-permute-start.4 = (bf16[640,512]{1,0:T(8,128)(2,1)S(1)}, bf16[640,512]{1,0:T(8,128)(2,1)S(1)}, u32[]{:S(2)}, u32[]{:S(2)}) collective-permute-start(bf16[640,512]{1,0:T(8,128)(2,1)S(1)} %get-tuple-element.27.own), channel_id=1, source_target_pairs={{0,12},{1,13},{2,14},{3,15},{4,0},{5,1},{6,2},{7,3},{8,4},{9,5},{1... | collective-permute-start | bytes 1966088 | tf_op jit(solution)/shard_map/ppermute | solution.py:289
  31.0 22.9 %collective-permute-start.3 = (bf16[640,512]{1,0:T(8,128)(2,1)S(1)}, bf16[640,512]{1,0:T(8,128)(2,1)S(1)}, u32[]{:S(2)}, u32[]{:S(2)}) collective-permute-start(bf16[640,512]{1,0:T(8,128)(2,1)S(1)} %get-tuple-element.27.own), channel_id=1, source_target_pairs={{0,4},{1,5},{2,6},{3,7},{4,8},{5,9},{6,10},{7,11},{8,12},{9,13},{1... | collective-permute-start | bytes 1966088 | tf_op jit(solution)/shard_map/ppermute | solution.py:289
  32.4 11.4 %collective-permute-start.7 = (bf16[4,64,896]{2,1,0:T(8,128)(2,1)S(1)}, bf16[4,64,896]{2,1,0:T(8,128)(2,1)S(1)}, u32[]{:S(2)}, u32[]{:S(2)}) collective-permute-start(bf16[4,64,896]{2,1,0:T(8,128)(2,1)S(1)} %pad_maximum_fusion.1), channel_id=1, source_target_pairs={{0,2},{1,3},{2,0},{3,1},{4,6},{5,7},{6,4},{7,5},{8,10},{9,11},{10,... | collective-permute-start | bytes 1376264 | tf_op jit(solution)/shard_map/ppermute | solution.py:289
  38.5 15.5 %collective-permute-start.6 = (bf16[368,512]{1,0:T(8,128)(2,1)S(1)}, bf16[368,512]{1,0:T(8,128)(2,1)S(1)}, u32[]{:S(2)}, u32[]{:S(2)}) collective-permute-start(bf16[368,512]{1,0:T(8,128)(2,1)S(1)} %collective-permute-done.5.same_ref), channel_id=1, source_target_pairs={{0,2},{1,3},{2,0},{3,1},{4,6},{5,7},{6,4},{7,5},{8,10},{9,11},{10,... | collective-permute-start | bytes 1130504 | tf_op jit(solution)/shard_map/ppermute | solution.py:289
  54.7 7.0 %collective-permute-start.8 = (bf16[2560,512]{1,0:T(8,128)(2,1)S(1)}, bf16[2560,512]{1,0:T(8,128)(2,1)S(1)}, u32[]{:S(2)}, u32[]{:S(2)}) collective-permute-start(bf16[2560,512]{1,0:T(8,128)(2,1)S(1)} %shard_map.52.rows_ref.own_ref), channel_id=1, source_target_pairs={{0,1},{1,0},{2,3},{3,2},{4,5},{5,4},{6,7},{7,6},{8,9},{9,8},{10,11... | collective-permute-start | bytes 7864328 | tf_op jit(solution)/shard_map/ppermute | solution.py:289
  56.0 5.7 %collective-permute-start.9 = (bf16[2,4,64,896]{3,2,1,0:T(8,128)(2,1)S(1)}, bf16[2,4,64,896]{3,2,1,0:T(8,128)(2,1)S(1)}, u32[]{:S(2)}, u32[]{:S(2)}) collective-permute-start(bf16[2,4,64,896]{3,2,1,0:T(8,128)(2,1)S(1)} %pad_maximum_fusion.o_own_ref), channel_id=1, source_target_pairs={{0,1},{1,0},{2,3},{3,2},{4,5},{5,4},{6,7},{7,6},{8,9},{9,8},{10,11... | collective-permute-start | bytes 2752520 | tf_op jit(solution)/shard_map/ppermute | solution.py:289

commit v5 on v4

--- a/solution.py
+++ b/solution.py
@@ -23,7 +23,7 @@
 ROWS = Q_ALL + 2 * F * L_BLOCK
 D_PART = 448
 bf16 = jnp.bfloat16
-PACK_MIB = 56
+PACK_MIB = 24
 EXTRA = 48
 VMEM = pl.BlockSpec(memory_space=pltpu.VMEM)
 ANY = pl.BlockSpec(memory_space=pl.ANY)
@@ -46,33 +46,25 @@
     return pltpu.CompilerParams(vmem_limit_bytes=mib * 2**20)
 
 
-def pack_kernel(q_hbm, kv_hbm, o_hbm, out_ref, *refs):
-    o_refs, (q_ref, kv_ref, sems) = refs[:X], refs[X:]
-    kv_copy = pltpu.make_async_copy(kv_hbm, kv_ref, sems.at[0])
-    q_copy = pltpu.make_async_copy(q_hbm, q_ref, sems.at[1])
-    kv_copy.start()
-    q_copy.start()
+def pack_kernel(q_ref, kv_ref, o_hbm, out_ref, *refs):
+    o_refs, sems = refs[:X], refs[X]
     copies = []
     o_cols = o_hbm.shape[1] // X
     for d in range(X):
         at = pl.multiple_of(lax.rem(lax.axis_index("x") + d, X) * o_cols, 128)
         copies.append(
-            pltpu.make_async_copy(o_hbm.at[:, pl.ds(at, o_cols)], o_refs[d], sems.at[2 + d])
+            pltpu.make_async_copy(o_hbm.at[:, pl.ds(at, o_cols)], o_refs[d], sems.at[d])
         )
         copies[d].start()
-    kv_copy.wait()
     for n in range(F * C):
-        for z in range(ZH):
-            at = (n // C * ZH + z) * C + n % C
+        first = n // C * (ZH * C) + n % C
+        q_lanes = slice(n * WIDE, (n + 1) * WIDE)
+        for at in (first, first + C):
+            out_ref[at, :Q_ROWS, :WIDE] = q_ref[:, q_lanes]
             out_ref[at, Q_ROWS:, :WIDE] = kv_ref[:, n * 1024 : n * 1024 + WIDE]
             for j in range(4):
                 lane = n * 1024 + WIDE + j * 128
                 out_ref[at, j * 4 : (j + 1) * 4, WIDE:] = kv_ref[:, lane : lane + 128]
-    q_copy.wait()
-    for n in range(F * C):
-        for z in range(ZH):
-            at = (n // C * ZH + z) * C + n % C
-            out_ref[at, :Q_ROWS, :WIDE] = q_ref[:, n * WIDE : (n + 1) * WIDE]
     for copy in copies:
         copy.wait()
 
@@ -81,15 +73,11 @@
     o_cols = o.shape[1] // X
     out = pl.pallas_call(
         pack_kernel,
-        in_specs=[ANY] * 3,
+        in_specs=[VMEM, VMEM, ANY],
         out_specs=[VMEM] * (X + 1),
         out_shape=[jax.ShapeDtypeStruct((F * ZH * C, 16, 640), bf16)]
         + [jax.ShapeDtypeStruct((o.shape[0], o_cols), bf16)] * X,
-        scratch_shapes=[
-            pltpu.VMEM(q.shape, bf16),
-            pltpu.VMEM(kv.shape, bf16),
-            pltpu.SemaphoreType.DMA((2 + X,)),
-        ],
+        scratch_shapes=[pltpu.SemaphoreType.DMA((X,))],
         compiler_params=limit(PACK_MIB),
         cost_estimate=COST,
     )(q, kv, o)

time: 66.1 us -> 67.2 us (1.017)
  local copies, waits for them, and re-layouts: 1.05 us -> 3.12 us
  Pallas kernels: 10.9 us -> 9.55 us
  waiting for transfers between devices: 27.4 us -> 28.2 us
    unnamed x0 -> x6, local copies, waits for them, and re-layouts: none -> 3.03 us
    pallas_call x1, Pallas kernels: 2.52 us -> 1.14 us  [pack(): pl.pallas_call(pack_kernel, in_specs=[VMEM, VMEM, ANY], out_specs=[VMEM]...]
    another operation x2, local copies, waits for them, and re-layouts: 1.05 us -> 0.1 us  [on_device(): jnp.stack([lax.dynamic_slice_in_dim(o, z * (2 * D_PART), 2 * D_PART, 1) f...]
    ppermute x10, waiting for transfers between devices: 27.4 us -> 28.2 us  [on_device(): over = lambda a, *d: lax.ppermute(a, BULK, shifts(*d))]
  transfers between devices with their start and end apart: 11 -> 11, of which waited for: 7 -> 7; matrix products, arithmetic and copies ran while one was open for 3% -> 1% of each run, Pallas kernels for 5% -> 5%
where the time goes in v5:
time: 67.2 us; the launch traced here: 66.9 us
  waiting for transfers between devices  28.2 us (42%)
  starting transfers between devices  24.4 us (36%)
  Pallas kernels  9.55 us (14%)
  local copies, waits for them, and re-layouts  3.12 us (5%)
  other arithmetic  0.85 us (1%)
  between operations  0.79 us (1%)
    ppermute x10, waiting for transfers between devices, on_device(): over = lambda a, *d: lax.ppermute(a, BULK, shifts(*d))  28.2 us
    ppermute x10, starting transfers between devices, on_device(): over = lambda a, *d: lax.ppermute(a, BULK, shifts(*d))  14.8 us
    all_to_all x1, starting transfers between devices, on_device(): lax.all_to_all(packed, OWNERS, split_axis=0, concat_axis=0, tiled=True)  9.61 us
    pallas_call x1, Pallas kernels, rest(): pl.pallas_call(rest_kernel, in_specs=[VMEM] * 4 + [ANY], out_specs=[ANY,...  4.21 us
    unnamed x6, local copies, waits for them, and re-layouts  3.03 us
    pallas_call x1, Pallas kernels, query(): pl.pallas_call(query_kernel, in_specs=[VMEM], out_specs=ANY, scratch_shap...  3.02 us
  transfers between devices with their start and end apart: 11, of which 7 were waited for; matrix products, arithmetic and copies ran while one was open for 1% of the time, Pallas kernels for 5%

profile of v5, /device:TPU:1, one launch (start us, length us, event | category | flops | bytes accessed | tf_op | source)
XLA Modules:
  0.0 66.9 jit_solution(6349506565337379451)
XLA Ops:
  0.6 1.2 %copy-done = bf16[64,7168]{1,0:T(8,128)(2,1)S(1)} copy-done((bf16[64,7168]{1,0:T(8,128)(2,1)S(1)}, bf16[64,7168]{1,0:T(8,128)(2,1)}, u32[]{:S(2)}) %copy-start) | copy-done | bytes 917528
  1.8 0.9 %copy-done.1 = bf16[12,8192]{1,0:T(8,128)(2,1)S(1)} copy-done((bf16[12,8192]{1,0:T(8,128)(2,1)S(1)}, bf16[12,8192]{1,0:T(8,128)(2,1)}, u32[]{:S(2)}) %copy-start.1) | copy-done | bytes 196632
  2.8 0.9 %copy-done.2 = bf16[4,16384]{1,0:T(4,128)(2,1)S(1)} copy-done((bf16[4,16384]{1,0:T(4,128)(2,1)S(1)}, bf16[4,16384]{1,0:T(4,128)(2,1)}, u32[]{:S(2)}) %copy-start.2) | copy-done | bytes 131096
  3.7 1.1 %shard_map.50 = (bf16[32,16,640]{2,1,0:T(8,128)(2,1)}, bf16[64,1792]{1,0:T(8,128)(2,1)S(1)}, bf16[64,1792]{1,0:T(8,128)(2,1)S(1)}, bf16[64,1792]{1,0:T(8,128)(2,1)S(1)}, bf16[64,1792]{1,0:T(8,128)(2,1)S(1)}) custom-call(bf16[12,8192]{1,0:T(8,128)(2,1)S(1)} %copy-done.1, bf16[4,16384]{1,0:T(4,128)(2,1)S(1)} %copy-done.2, bf16[64,7168]{1,0:T(8,128)(2,1)S(1)} %copy-done), custom_call_target="tpu_custom_call" | custom-call | flops 1024 | bytes 1024 | tf_op jit(solution)/shard_map/pallas_call | solution.py:74
  4.8 9.6 %all-to-all-start = ((bf16[32,16,640]{2,1,0:T(8,128)(2,1)}), bf16[32,16,640]{2,1,0:T(8,128)(2,1)S(1)}, u32[]{:S(2)}, u32[]{:S(2)}) async-start(bf16[32,16,640]{2,1,0:T(8,128)(2,1)} %get-tuple-element.21), calls=%async_computation | async-start | bytes 1310720 | tf_op jit(solution)/shard_map/all_to_all | solution.py:281
  14.4 1.3 %collective-permute-start = (bf16[64,1792]{1,0:T(8,128)(2,1)S(1)}, bf16[64,1792]{1,0:T(8,128)(2,1)S(1)}, u32[]{:S(2)}, u32[]{:S(2)}) collective-permute-start(bf16[64,1792]{1,0:T(8,128)(2,1)S(1)} %get-tuple-element.23), channel_id=1, source_target_pairs={{0,4},{1,5},{2,6},{3,7},{4,8},{5,9},{6,10},{7,11},{8,12},{9,13},{1... | collective-permute-start | bytes 688136 | tf_op jit(solution)/shard_map/ppermute | solution.py:277
  15.7 2.5 %collective-permute-start.1 = (bf16[64,1792]{1,0:T(8,128)(2,1)S(1)}, bf16[64,1792]{1,0:T(8,128)(2,1)S(1)}, u32[]{:S(2)}, u32[]{:S(2)}) collective-permute-start(bf16[64,1792]{1,0:T(8,128)(2,1)S(1)} %get-tuple-element.24), channel_id=1, source_target_pairs={{0,8},{1,9},{2,10},{3,11},{4,12},{5,13},{6,14},{7,15},{8,0},{9,1},... | collective-permute-start | bytes 688136 | tf_op jit(solution)/shard_map/ppermute | solution.py:277
  18.2 1.2 %collective-permute-start.2 = (bf16[64,1792]{1,0:T(8,128)(2,1)S(1)}, bf16[64,1792]{1,0:T(8,128)(2,1)S(1)}, u32[]{:S(2)}, u32[]{:S(2)}) collective-permute-start(bf16[64,1792]{1,0:T(8,128)(2,1)S(1)} %get-tuple-element.25), channel_id=1, source_target_pairs={{0,12},{1,13},{2,14},{3,15},{4,0},{5,1},{6,2},{7,3},{8,4},{9,5},{1... | collective-permute-start | bytes 688136 | tf_op jit(solution)/shard_map/ppermute | solution.py:277
  19.4 0.1 fusion.left_ref
  19.5 0.1 fusion.3.half_left_ref
  19.6 0.1 fusion.4.half_right_ref
  19.7 0.1 fusion.1.right_ref
  19.8 2.9 %collective-permute-done = bf16[64,1792]{1,0:T(8,128)(2,1)S(1)} collective-permute-done((bf16[64,1792]{1,0:T(8,128)(2,1)S(1)}, bf16[64,1792]{1,0:T(8,128)(2,1)S(1)}, u32[]{:S(2)}, u32[]{:S(2)}) %collective-permute-start) | collective-permute-done | bytes 229408 | tf_op jit(solution)/shard_map/ppermute | solution.py:277
  22.7 5.9 %collective-permute-done.1 = bf16[64,1792]{1,0:T(8,128)(2,1)S(1)} collective-permute-done((bf16[64,1792]{1,0:T(8,128)(2,1)S(1)}, bf16[64,1792]{1,0:T(8,128)(2,1)S(1)}, u32[]{:S(2)}, u32[]{:S(2)}) %collective-permute-start.1) | collective-permute-done | bytes 229408 | tf_op jit(solution)/shard_map/ppermute | solution.py:277
  28.6 0.5 shard_map.51
  29.1 2.2 %collective-permute-start.5 = (bf16[368,512]{1,0:T(8,128)(2,1)S(1)}, bf16[368,512]{1,0:T(8,128)(2,1)S(1)}, u32[]{:S(2)}, u32[]{:S(2)}) collective-permute-start(bf16[368,512]{1,0:T(8,128)(2,1)S(1)} %get-tuple-element.28), channel_id=1, source_target_pairs={{0,8},{1,9},{2,10},{3,11},{4,12},{5,13},{6,14},{7,15},{8,0},{9,1},... | collective-permute-start | bytes 1130504 | tf_op jit(solution)/shard_map/ppermute | solution.py:277
  31.2 1.2 %collective-permute-start.4 = (bf16[640,512]{1,0:T(8,128)(2,1)S(1)}, bf16[640,512]{1,0:T(8,128)(2,1)S(1)}, u32[]{:S(2)}, u32[]{:S(2)}) collective-permute-start(bf16[640,512]{1,0:T(8,128)(2,1)S(1)} %get-tuple-element.27.own), channel_id=1, source_target_pairs={{0,12},{1,13},{2,14},{3,15},{4,0},{5,1},{6,2},{7,3},{8,4},{9,5},{1... | collective-permute-start | bytes 1966088 | tf_op jit(solution)/shard_map/ppermute | solution.py:277
  32.5 0.2 collective-permute-start.3
  32.9 2.9 %collective-permute-start.7 = (bf16[4,64,896]{2,1,0:T(8,128)(2,1)S(1)}, bf16[4,64,896]{2,1,0:T(8,128)(2,1)S(1)}, u32[]{:S(2)}, u32[]{:S(2)}) collective-permute-start(bf16[4,64,896]{2,1,0:T(8,128)(2,1)S(1)} %pad_maximum_fusion.1), channel_id=1, source_target_pairs={{0,2},{1,3},{2,0},{3,1},{4,6},{5,7},{6,4},{7,5},{8,10},{9,11},{10,... | collective-permute-start | bytes 1376264 | tf_op jit(solution)/shard_map/ppermute | solution.py:277
  35.7 4.2 %collective-permute-done.5.same_ref = bf16[368,512]{1,0:T(8,128)(2,1)S(1)} collective-permute-done((bf16[368,512]{1,0:T(8,128)(2,1)S(1)}, bf16[368,512]{1,0:T(8,128)(2,1)S(1)}, u32[]{:S(2)}, u32[]{:S(2)}) %collective-permute-start.5) | collective-permute-done | bytes 376864 | tf_op jit(solution)/shard_map/ppermute | solution.py:277
  39.9 2.6 %collective-permute-start.6 = (bf16[368,512]{1,0:T(8,128)(2,1)S(1)}, bf16[368,512]{1,0:T(8,128)(2,1)S(1)}, u32[]{:S(2)}, u32[]{:S(2)}) collective-permute-start(bf16[368,512]{1,0:T(8,128)(2,1)S(1)} %collective-permute-done.5.same_ref), channel_id=1, source_target_pairs={{0,2},{1,3},{2,0},{3,1},{4,6},{5,7},{6,4},{7,5},{8,10},{9,11},{10,... | collective-permute-start | bytes 1130504 | tf_op jit(solution)/shard_map/ppermute | solution.py:277
  42.6 0.1 fusion.2.by_q_ref
  42.7 1.6 %collective-permute-done.7 = bf16[4,64,896]{2,1,0:T(8,128)(2,1)S(1)} collective-permute-done((bf16[4,64,896]{2,1,0:T(8,128)(2,1)S(1)}, bf16[4,64,896]{2,1,0:T(8,128)(2,1)S(1)}, u32[]{:S(2)}, u32[]{:S(2)}) %collective-permute-start.7) | collective-permute-done | bytes 458784 | tf_op jit(solution)/shard_map/ppermute | solution.py:277
  44.3 10.4 %collective-permute-done.4.left = bf16[640,512]{1,0:T(8,128)(2,1)S(1)} collective-permute-done((bf16[640,512]{1,0:T(8,128)(2,1)S(1)}, bf16[640,512]{1,0:T(8,128)(2,1)S(1)}, u32[]{:S(2)}, u32[]{:S(2)}) %collective-permute-start.4) | collective-permute-done | bytes 655392 | tf_op jit(solution)/shard_map/ppermute | solution.py:277
  54.7 0.7 collective-permute-done.3.right
  55.4 0.7 %shard_map.52.rows_ref.own_ref = bf16[2560,512]{1,0:T(8,128)(2,1)S(1)} custom-call(bf16[640,512]{1,0:T(8,128)(2,1)S(1)} %get-tuple-element.27.own, bf16[640,512]{1,0:T(8,128)(2,1)S(1)} %collective-permute-done.3.right, bf16[640,512]{1,0:T(8,128)(2,1)S(1)} %collective-permute-done.4.left, bf16[368,512]{1,0:T(8,128)(2,1)S(1)} %collective-permute-done.5.same_ref, ...), custom_call_target="tpu_custom_call" | custom-call | flops 1024 | bytes 1024 | tf_op jit(solution)/shard_map/pallas_call | solution.py:169
  56.1 0.8 %collective-permute-start.8 = (bf16[2560,512]{1,0:T(8,128)(2,1)S(1)}, bf16[2560,512]{1,0:T(8,128)(2,1)S(1)}, u32[]{:S(2)}, u32[]{:S(2)}) collective-permute-start(bf16[2560,512]{1,0:T(8,128)(2,1)S(1)} %shard_map.52.rows_ref.own_ref), channel_id=1, source_target_pairs={{0,1},{1,0},{2,3},{3,2},{4,5},{5,4},{6,7},{7,6},{8,9},{9,8},{10,11... | collective-permute-start | bytes 7864328 | tf_op jit(solution)/shard_map/ppermute | solution.py:277
  56.9 0.1 pad_maximum_fusion.o_own_ref
  57.0 0.1 collective-permute-start.9
  57.1 3.0 %shard_map.53._ = bf16[8,8,4,48,512]{4,3,2,1,0:T(8,128)(2,1)} custom-call(bf16[2560,512]{1,0:T(8,128)(2,1)S(1)} %shard_map.52.rows_ref.own_ref), custom_call_target="tpu_custom_call" | custom-call | flops 1024 | bytes 1024 | tf_op jit(solution)/shard_map/pallas_call | solution.py:213
  60.2 2.5 %collective-permute-done.9.o_other_ref = bf16[2,4,64,896]{3,2,1,0:T(8,128)(2,1)S(1)} collective-permute-done((bf16[2,4,64,896]{3,2,1,0:T(8,128)(2,1)S(1)}, bf16[2,4,64,896]{3,2,1,0:T(8,128)(2,1)S(1)}, u32[]{:S(2)}, u32[]{:S(2)}) %collective-permute-start.9) | collective-permute-done | bytes 917536 | tf_op jit(solution)/shard_map/ppermute | solution.py:277
  62.7 4.2 %shard_map.54 = (bf16[8,8,4,48,512]{4,3,2,1,0:T(8,128)(2,1)}, bf16[8,448,512]{2,1,0:T(8,128)(2,1)}) custom-call(bf16[2560,512]{1,0:T(8,128)(2,1)S(1)} %shard_map.52.rows_ref.own_ref, bf16[2560,512]{1,0:T(8,128)(2,1)S(1)} %collective-permute-done.8.other_ref, bf16[2,4,64,896]{3,2,1,0:T(8,128)(2,1)S(1)} %pad_maximum_fusion.o_own_ref, ...), custom_call_target="tpu_custom_call", output_to_operand_aliasing={{0}: (4, {})} | custom-call | flops 1024 | bytes 1024 | tf_op jit(solution)/shard_map/pallas_call | solution.py:255
  (16 shorter events, 0.4 us)
Async XLA Ops:
  0.6 1.2 %copy-start = (bf16[64,7168]{1,0:T(8,128)(2,1)S(1)}, bf16[64,7168]{1,0:T(8,128)(2,1)}, u32[]{:S(2)}) copy-start(bf16[64,7168]{1,0:T(8,128)(2,1)} %o_hbm.1) | copy-start | bytes 2752516
  1.8 0.9 %copy-start.1 = (bf16[12,8192]{1,0:T(8,128)(2,1)S(1)}, bf16[12,8192]{1,0:T(8,128)(2,1)}, u32[]{:S(2)}) copy-start(bf16[12,8192]{1,0:T(8,128)(2,1)} %q_ref.1) | copy-start | bytes 589828
  2.8 0.9 %copy-start.2 = (bf16[4,16384]{1,0:T(4,128)(2,1)S(1)}, bf16[4,16384]{1,0:T(4,128)(2,1)}, u32[]{:S(2)}) copy-start(bf16[4,16384]{1,0:T(4,128)(2,1)} %kv_ref.1) | copy-start | bytes 393220
  4.8 23.8 %all-to-all-start = ((bf16[32,16,640]{2,1,0:T(8,128)(2,1)}), bf16[32,16,640]{2,1,0:T(8,128)(2,1)S(1)}, u32[]{:S(2)}, u32[]{:S(2)}) async-start(bf16[32,16,640]{2,1,0:T(8,128)(2,1)} %get-tuple-element.21), calls=%async_computation | async-start | bytes 1310720 | tf_op jit(solution)/shard_map/all_to_all | solution.py:281
  14.4 8.3 %collective-permute-start = (bf16[64,1792]{1,0:T(8,128)(2,1)S(1)}, bf16[64,1792]{1,0:T(8,128)(2,1)S(1)}, u32[]{:S(2)}, u32[]{:S(2)}) collective-permute-start(bf16[64,1792]{1,0:T(8,128)(2,1)S(1)} %get-tuple-element.23), channel_id=1, source_target_pairs={{0,4},{1,5},{2,6},{3,7},{4,8},{5,9},{6,10},{7,11},{8,12},{9,13},{1... | collective-permute-start | bytes 688136 | tf_op jit(solution)/shard_map/ppermute | solution.py:277
  15.7 12.9 %collective-permute-start.1 = (bf16[64,1792]{1,0:T(8,128)(2,1)S(1)}, bf16[64,1792]{1,0:T(8,128)(2,1)S(1)}, u32[]{:S(2)}, u32[]{:S(2)}) collective-permute-start(bf16[64,1792]{1,0:T(8,128)(2,1)S(1)} %get-tuple-element.24), channel_id=1, source_target_pairs={{0,8},{1,9},{2,10},{3,11},{4,12},{5,13},{6,14},{7,15},{8,0},{9,1},... | collective-permute-start | bytes 688136 | tf_op jit(solution)/shard_map/ppermute | solution.py:277
  18.2 10.4 %collective-permute-start.2 = (bf16[64,1792]{1,0:T(8,128)(2,1)S(1)}, bf16[64,1792]{1,0:T(8,128)(2,1)S(1)}, u32[]{:S(2)}, u32[]{:S(2)}) collective-permute-start(bf16[64,1792]{1,0:T(8,128)(2,1)S(1)} %get-tuple-element.25), channel_id=1, source_target_pairs={{0,12},{1,13},{2,14},{3,15},{4,0},{5,1},{6,2},{7,3},{8,4},{9,5},{1... | collective-permute-start | bytes 688136 | tf_op jit(solution)/shard_map/ppermute | solution.py:277
  29.1 10.8 %collective-permute-start.5 = (bf16[368,512]{1,0:T(8,128)(2,1)S(1)}, bf16[368,512]{1,0:T(8,128)(2,1)S(1)}, u32[]{:S(2)}, u32[]{:S(2)}) collective-permute-start(bf16[368,512]{1,0:T(8,128)(2,1)S(1)} %get-tuple-element.28), channel_id=1, source_target_pairs={{0,8},{1,9},{2,10},{3,11},{4,12},{5,13},{6,14},{7,15},{8,0},{9,1},... | collective-permute-start | bytes 1130504 | tf_op jit(solution)/shard_map/ppermute | solution.py:277
  31.2 23.5 %collective-permute-start.4 = (bf16[640,512]{1,0:T(8,128)(2,1)S(1)}, bf16[640,512]{1,0:T(8,128)(2,1)S(1)}, u32[]{:S(2)}, u32[]{:S(2)}) collective-permute-start(bf16[640,512]{1,0:T(8,128)(2,1)S(1)} %get-tuple-element.27.own), channel_id=1, source_target_pairs={{0,12},{1,13},{2,14},{3,15},{4,0},{5,1},{6,2},{7,3},{8,4},{9,5},{1... | collective-permute-start | bytes 1966088 | tf_op jit(solution)/shard_map/ppermute | solution.py:277
  32.5 22.9 %collective-permute-start.3 = (bf16[640,512]{1,0:T(8,128)(2,1)S(1)}, bf16[640,512]{1,0:T(8,128)(2,1)S(1)}, u32[]{:S(2)}, u32[]{:S(2)}) collective-permute-start(bf16[640,512]{1,0:T(8,128)(2,1)S(1)} %get-tuple-element.27.own), channel_id=1, source_target_pairs={{0,4},{1,5},{2,6},{3,7},{4,8},{5,9},{6,10},{7,11},{8,12},{9,13},{1... | collective-permute-start | bytes 1966088 | tf_op jit(solution)/shard_map/ppermute | solution.py:277
  32.9 11.4 %collective-permute-start.7 = (bf16[4,64,896]{2,1,0:T(8,128)(2,1)S(1)}, bf16[4,64,896]{2,1,0:T(8,128)(2,1)S(1)}, u32[]{:S(2)}, u32[]{:S(2)}) collective-permute-start(bf16[4,64,896]{2,1,0:T(8,128)(2,1)S(1)} %pad_maximum_fusion.1), channel_id=1, source_target_pairs={{0,2},{1,3},{2,0},{3,1},{4,6},{5,7},{6,4},{7,5},{8,10},{9,11},{10,... | collective-permute-start | bytes 1376264 | tf_op jit(solution)/shard_map/ppermute | solution.py:277
  39.9 15.5 %collective-permute-start.6 = (bf16[368,512]{1,0:T(8,128)(2,1)S(1)}, bf16[368,512]{1,0:T(8,128)(2,1)S(1)}, u32[]{:S(2)}, u32[]{:S(2)}) collective-permute-start(bf16[368,512]{1,0:T(8,128)(2,1)S(1)} %collective-permute-done.5.same_ref), channel_id=1, source_target_pairs={{0,2},{1,3},{2,0},{3,1},{4,6},{5,7},{6,4},{7,5},{8,10},{9,11},{10,... | collective-permute-start | bytes 1130504 | tf_op jit(solution)/shard_map/ppermute | solution.py:277
  56.1 6.6 %collective-permute-start.8 = (bf16[2560,512]{1,0:T(8,128)(2,1)S(1)}, bf16[2560,512]{1,0:T(8,128)(2,1)S(1)}, u32[]{:S(2)}, u32[]{:S(2)}) collective-permute-start(bf16[2560,512]{1,0:T(8,128)(2,1)S(1)} %shard_map.52.rows_ref.own_ref), channel_id=1, source_target_pairs={{0,1},{1,0},{2,3},{3,2},{4,5},{5,4},{6,7},{7,6},{8,9},{9,8},{10,11... | collective-permute-start | bytes 7864328 | tf_op jit(solution)/shard_map/ppermute | solution.py:277
  57.0 5.7 %collective-permute-start.9 = (bf16[2,4,64,896]{3,2,1,0:T(8,128)(2,1)S(1)}, bf16[2,4,64,896]{3,2,1,0:T(8,128)(2,1)S(1)}, u32[]{:S(2)}, u32[]{:S(2)}) collective-permute-start(bf16[2,4,64,896]{3,2,1,0:T(8,128)(2,1)S(1)} %pad_maximum_fusion.o_own_ref), channel_id=1, source_target_pairs={{0,1},{1,0},{2,3},{3,2},{4,5},{5,4},{6,7},{7,6},{8,9},{9,8},{10,11... | collective-permute-start | bytes 2752520 | tf_op jit(solution)/shard_map/ppermute | solution.py:277

commit v6 on v4

--- a/solution.py
+++ b/solution.py
@@ -143,7 +143,9 @@
     )(packed, *select(4, 0), *select(2, zh * 2))
 
 
-def sort_kernel(own, right, left, same_ref, cross_ref, by_q_ref, by_l_ref, out, far, kv):
+def sort_kernel(own, right, left, same_ref, cross_ref, by_q_ref, by_l_ref, o_ref, out, o_out, far, kv):
+    there = pl.ds(pl.multiple_of((1 - lax.axis_index("c")) * 384, 128), 512)
+    o_out[...] = o_ref[:, :, :, there]
     half_q, half_l = Q_ALL // 4, F * L_BLOCK // 2
     for g in range(2):
         at = slice(g * half_q, (g + 1) * half_q)
@@ -177,14 +179,17 @@
     return (source[:, None] == row[None, :]).astype(bf16)
 
 
-def sort_rows(zh, own, right, left, same, cross):
+def sort_rows(zh, own, right, left, same, cross, o_own):
     return pl.pallas_call(
         sort_kernel,
-        out_shape=jax.ShapeDtypeStruct((2 * KVL + X * Q_ALL, WIDE), bf16),
+        out_shape=[
+            jax.ShapeDtypeStruct((2 * KVL + X * Q_ALL, WIDE), bf16),
+            jax.ShapeDtypeStruct((ZH, X, 64, 512), bf16),
+        ],
         scratch_shapes=[pltpu.VMEM((ROWS, WIDE), bf16), pltpu.VMEM((KVL, 1024), bf16)],
         compiler_params=limit(12),
         cost_estimate=COST,
-    )(own, right, left, same, cross, interleave(F // 2, 24, zh), interleave(F, 8, zh))
+    )(own, right, left, same, cross, interleave(F // 2, 24, zh), interleave(F, 8, zh), o_own)
 
 
 def sender(sems):
@@ -251,7 +256,7 @@
             z = lax.rem(zh + k, 2)
             at = n * HALF + k
             heads[at, own_at, :] = o_own_ref[z, d, :, lanes]
-            heads[at, other_at, :] = o_other_ref[z, d, :, lanes]
+            heads[at, other_at, :] = o_other_ref[z, d]
         for k in range(HALF):
             at = n * HALF + k
             value = rows_ref[KVL : 2 * KVL, k * VD : (k + 1) * VD]
@@ -305,8 +310,8 @@
     near, same, cross, o_z = lax.optimization_barrier((near, same, cross, o_z))
 
     o_own = jnp.stack([half(zh), o_z])
-    o_other = over(o_own, *core)
-    rows = sort_rows(zh, own, *near, same, cross)
+    rows, o_window = sort_rows(zh, own, *near, same, cross, o_own)
+    o_other = over(o_window, *core)
     rows_other = over(rows, *core)
     q_out = query(rows)
     q_out, d_out = rest(rows, rows_other, o_own, o_other, q_out)

time: 66.1 us -> 65.8 us (level)
  no operation moved by 1% of the time
where the time goes in v6:
time: 65.8 us; the launch traced here: 65.5 us
  waiting for transfers between devices  26.9 us (41%)
  starting transfers between devices  25 us (38%)
  Pallas kernels  10.9 us (17%)
  local copies, waits for them, and re-layouts  1.05 us (2%)
  other arithmetic  0.85 us (1%)
  between operations  0.78 us (1%)
    ppermute x10, waiting for transfers between devices, on_device(): over = lambda a, *d: lax.ppermute(a, BULK, shifts(*d))  26.9 us
    ppermute x10, starting transfers between devices, on_device(): over = lambda a, *d: lax.ppermute(a, BULK, shifts(*d))  15.4 us
    all_to_all x1, starting transfers between devices, on_device(): lax.all_to_all(packed, OWNERS, split_axis=0, concat_axis=0, tiled=True)  9.61 us
    pallas_call x1, Pallas kernels, rest(): pl.pallas_call(rest_kernel, in_specs=[VMEM] * 4 + [ANY], out_specs=[ANY,...  4.2 us
    pallas_call x1, Pallas kernels, query(): pl.pallas_call(query_kernel, in_specs=[VMEM], out_specs=ANY, scratch_shap...  3.02 us
    pallas_call x1, Pallas kernels, pack(): pl.pallas_call(pack_kernel, in_specs=[ANY] * 3, out_specs=[VMEM] * (X + 1...  2.53 us
  transfers between devices with their start and end apart: 11, of which 7 were waited for; matrix products, arithmetic and copies ran while one was open for 3% of the time, Pallas kernels for 5%

profile of v6, /device:TPU:1, one launch (start us, length us, event | category | flops | bytes accessed | tf_op | source)
XLA Modules:
  0.0 65.5 jit_solution(17331255151809674099)
XLA Ops:
  0.6 2.5 %shard_map.50 = (bf16[32,16,640]{2,1,0:T(8,128)(2,1)}, bf16[64,1792]{1,0:T(8,128)(2,1)}, bf16[64,1792]{1,0:T(8,128)(2,1)}, bf16[64,1792]{1,0:T(8,128)(2,1)}, bf16[64,1792]{1,0:T(8,128)(2,1)}) custom-call(bf16[12,8192]{1,0:T(8,128)(2,1)} %q_hbm.1, bf16[4,16384]{1,0:T(4,128)(2,1)} %kv_hbm.1, bf16[64,7168]{1,0:T(8,128)(2,1)} %o_hbm.1), custom_call_target="tpu_custom_call" | custom-call | flops 1024 | bytes 1024 | tf_op jit(solution)/shard_map/pallas_call | solution.py:82
  3.2 9.6 %all-to-all-start = ((bf16[32,16,640]{2,1,0:T(8,128)(2,1)}), bf16[32,16,640]{2,1,0:T(8,128)(2,1)S(1)}, u32[]{:S(2)}, u32[]{:S(2)}) async-start(bf16[32,16,640]{2,1,0:T(8,128)(2,1)} %get-tuple-element.23), calls=%async_computation | async-start | bytes 1310720 | tf_op jit(solution)/shard_map/all_to_all | solution.py:298
  12.8 1.3 %collective-permute-start = (bf16[64,1792]{1,0:T(8,128)(2,1)}, bf16[64,1792]{1,0:T(8,128)(2,1)S(1)}, u32[]{:S(2)}, u32[]{:S(2)}) collective-permute-start(bf16[64,1792]{1,0:T(8,128)(2,1)} %get-tuple-element.25), channel_id=1, source_target_pairs={{0,4},{1,5},{2,6},{3,7},{4,8},{5,9},{6,10},{7,11},{8,12},{9,13},{1... | collective-permute-start | bytes 688136 | tf_op jit(solution)/shard_map/ppermute | solution.py:294
  14.1 2.5 %collective-permute-start.1 = (bf16[64,1792]{1,0:T(8,128)(2,1)}, bf16[64,1792]{1,0:T(8,128)(2,1)S(1)}, u32[]{:S(2)}, u32[]{:S(2)}) collective-permute-start(bf16[64,1792]{1,0:T(8,128)(2,1)} %get-tuple-element.26), channel_id=1, source_target_pairs={{0,8},{1,9},{2,10},{3,11},{4,12},{5,13},{6,14},{7,15},{8,0},{9,1},... | collective-permute-start | bytes 688136 | tf_op jit(solution)/shard_map/ppermute | solution.py:294
  16.5 1.2 %collective-permute-start.2 = (bf16[64,1792]{1,0:T(8,128)(2,1)}, bf16[64,1792]{1,0:T(8,128)(2,1)S(1)}, u32[]{:S(2)}, u32[]{:S(2)}) collective-permute-start(bf16[64,1792]{1,0:T(8,128)(2,1)} %get-tuple-element.27), channel_id=1, source_target_pairs={{0,12},{1,13},{2,14},{3,15},{4,0},{5,1},{6,2},{7,3},{8,4},{9,5},{1... | collective-permute-start | bytes 688136 | tf_op jit(solution)/shard_map/ppermute | solution.py:294
  17.7 0.1 fusion.3.half_left_ref
  17.8 0.1 fusion.4.half_right_ref
  17.9 0.1 fusion.left_ref
  18.0 0.1 fusion.1.right_ref
  18.1 3.1 %collective-permute-done = bf16[64,1792]{1,0:T(8,128)(2,1)S(1)} collective-permute-done((bf16[64,1792]{1,0:T(8,128)(2,1)}, bf16[64,1792]{1,0:T(8,128)(2,1)S(1)}, u32[]{:S(2)}, u32[]{:S(2)}) %collective-permute-start) | collective-permute-done | bytes 229408 | tf_op jit(solution)/shard_map/ppermute | solution.py:294
  21.3 5.9 %collective-permute-done.1 = bf16[64,1792]{1,0:T(8,128)(2,1)S(1)} collective-permute-done((bf16[64,1792]{1,0:T(8,128)(2,1)}, bf16[64,1792]{1,0:T(8,128)(2,1)S(1)}, u32[]{:S(2)}, u32[]{:S(2)}) %collective-permute-start.1) | collective-permute-done | bytes 229408 | tf_op jit(solution)/shard_map/ppermute | solution.py:294
  27.2 0.5 shard_map.51
  27.6 2.1 %collective-permute-start.5 = (bf16[368,512]{1,0:T(8,128)(2,1)S(1)}, bf16[368,512]{1,0:T(8,128)(2,1)S(1)}, u32[]{:S(2)}, u32[]{:S(2)}) collective-permute-start(bf16[368,512]{1,0:T(8,128)(2,1)S(1)} %get-tuple-element.30), channel_id=1, source_target_pairs={{0,8},{1,9},{2,10},{3,11},{4,12},{5,13},{6,14},{7,15},{8,0},{9,1},... | collective-permute-start | bytes 1130504 | tf_op jit(solution)/shard_map/ppermute | solution.py:294
  29.8 0.1 fusion.5.by_l_ref
  29.9 1.3 %collective-permute-start.4 = (bf16[640,512]{1,0:T(8,128)(2,1)S(1)}, bf16[640,512]{1,0:T(8,128)(2,1)S(1)}, u32[]{:S(2)}, u32[]{:S(2)}) collective-permute-start(bf16[640,512]{1,0:T(8,128)(2,1)S(1)} %get-tuple-element.29.own), channel_id=1, source_target_pairs={{0,12},{1,13},{2,14},{3,15},{4,0},{5,1},{6,2},{7,3},{8,4},{9,5},{1... | collective-permute-start | bytes 1966088 | tf_op jit(solution)/shard_map/ppermute | solution.py:294
  31.2 0.2 collective-permute-start.3
  31.4 1.0 %dynamic-slice_bitcast_fusion.2 = (bf16[1,64,896]{2,1,0:T(8,128)(2,1)S(1)}, bf16[1,64,896]{2,1,0:T(8,128)(2,1)S(1)}, bf16[1,64,896]{2,1,0:T(8,128)(2,1)S(1)}, bf16[1,64,896]{2,1,0:T(8,128)(2,1)S(1)}) fusion(bf16[64,1792]{1,0:T(8,128)(2,1)S(1)} %collective-permute-done, s32[]{:T(128)S(6)} %select_n.340, s32[]{:T(128)S(6)} %select_n.329, ...), kind=kLoop, calls=%fused_computation.15 | loop fusion | bytes 917512 | tf_op jit(solution)/shard_map/stack | solution.py:306
  32.5 0.1 pad_maximum_fusion.1
  32.6 2.9 %collective-permute-start.7 = (bf16[4,64,896]{2,1,0:T(8,128)(2,1)S(1)}, bf16[4,64,896]{2,1,0:T(8,128)(2,1)S(1)}, u32[]{:S(2)}, u32[]{:S(2)}) collective-permute-start(bf16[4,64,896]{2,1,0:T(8,128)(2,1)S(1)} %pad_maximum_fusion.1), channel_id=1, source_target_pairs={{0,2},{1,3},{2,0},{3,1},{4,6},{5,7},{6,4},{7,5},{8,10},{9,11},{10,... | collective-permute-start | bytes 1376264 | tf_op jit(solution)/shard_map/ppermute | solution.py:294
  35.4 3.1 %collective-permute-done.5.same_ref = bf16[368,512]{1,0:T(8,128)(2,1)S(1)} collective-permute-done((bf16[368,512]{1,0:T(8,128)(2,1)S(1)}, bf16[368,512]{1,0:T(8,128)(2,1)S(1)}, u32[]{:S(2)}, u32[]{:S(2)}) %collective-permute-start.5) | collective-permute-done | bytes 376864 | tf_op jit(solution)/shard_map/ppermute | solution.py:294
  38.5 2.6 %collective-permute-start.6 = (bf16[368,512]{1,0:T(8,128)(2,1)S(1)}, bf16[368,512]{1,0:T(8,128)(2,1)S(1)}, u32[]{:S(2)}, u32[]{:S(2)}) collective-permute-start(bf16[368,512]{1,0:T(8,128)(2,1)S(1)} %collective-permute-done.5.same_ref), channel_id=1, source_target_pairs={{0,2},{1,3},{2,0},{3,1},{4,6},{5,7},{6,4},{7,5},{8,10},{9,11},{10,... | collective-permute-start | bytes 1130504 | tf_op jit(solution)/shard_map/ppermute | solution.py:294
  41.1 0.1 fusion.2.by_q_ref
  41.3 2.7 %collective-permute-done.7 = bf16[4,64,896]{2,1,0:T(8,128)(2,1)S(1)} collective-permute-done((bf16[4,64,896]{2,1,0:T(8,128)(2,1)S(1)}, bf16[4,64,896]{2,1,0:T(8,128)(2,1)S(1)}, u32[]{:S(2)}, u32[]{:S(2)}) %collective-permute-start.7) | collective-permute-done | bytes 458784 | tf_op jit(solution)/shard_map/ppermute | solution.py:294
  44.0 9.3 %collective-permute-done.4.left = bf16[640,512]{1,0:T(8,128)(2,1)S(1)} collective-permute-done((bf16[640,512]{1,0:T(8,128)(2,1)S(1)}, bf16[640,512]{1,0:T(8,128)(2,1)S(1)}, u32[]{:S(2)}, u32[]{:S(2)}) %collective-permute-start.4) | collective-permute-done | bytes 655392 | tf_op jit(solution)/shard_map/ppermute | solution.py:294
  53.3 0.7 %collective-permute-done.3.right = bf16[640,512]{1,0:T(8,128)(2,1)S(1)} collective-permute-done((bf16[640,512]{1,0:T(8,128)(2,1)S(1)}, bf16[640,512]{1,0:T(8,128)(2,1)S(1)}, u32[]{:S(2)}, u32[]{:S(2)}) %collective-permute-start.3) | collective-permute-done | bytes 655392 | tf_op jit(solution)/shard_map/ppermute | solution.py:294
  54.0 0.1 pad_maximum_fusion.o_ref.o_own_ref
  54.1 0.7 %shard_map.52 = (bf16[2560,512]{1,0:T(8,128)(2,1)S(1)}, bf16[2,4,64,512]{3,2,1,0:T(8,128)(2,1)S(1)}) custom-call(bf16[640,512]{1,0:T(8,128)(2,1)S(1)} %get-tuple-element.29.own, bf16[640,512]{1,0:T(8,128)(2,1)S(1)} %collective-permute-done.3.right, bf16[640,512]{1,0:T(8,128)(2,1)S(1)} %collective-permute-done.4.left, ...), custom_call_target="tpu_custom_call" | custom-call | flops 1024 | bytes 1024 | tf_op jit(solution)/shard_map/pallas_call | solution.py:183
  54.8 1.3 %collective-permute-start.8 = (bf16[2560,512]{1,0:T(8,128)(2,1)S(1)}, bf16[2560,512]{1,0:T(8,128)(2,1)S(1)}, u32[]{:S(2)}, u32[]{:S(2)}) collective-permute-start(bf16[2560,512]{1,0:T(8,128)(2,1)S(1)} %get-tuple-element.40.rows_ref.own_ref), channel_id=1, source_target_pairs={{0,1},{1,0},{2,3},{3,2},{4,5},{5,4},{6,7},{7,6},{8,9},{9,8},{10,11... | collective-permute-start | bytes 7864328 | tf_op jit(solution)/shard_map/ppermute | solution.py:294
  56.1 0.1 collective-permute-start.9
  56.1 3.0 %shard_map.53._ = bf16[8,8,4,48,512]{4,3,2,1,0:T(8,128)(2,1)} custom-call(bf16[2560,512]{1,0:T(8,128)(2,1)S(1)} %get-tuple-element.40.rows_ref.own_ref), custom_call_target="tpu_custom_call" | custom-call | flops 1024 | bytes 1024 | tf_op jit(solution)/shard_map/pallas_call | solution.py:230
  59.2 2.2 %collective-permute-done.9.o_other_ref = bf16[2,4,64,512]{3,2,1,0:T(8,128)(2,1)S(1)} collective-permute-done((bf16[2,4,64,512]{3,2,1,0:T(8,128)(2,1)S(1)}, bf16[2,4,64,512]{3,2,1,0:T(8,128)(2,1)S(1)}, u32[]{:S(2)}, u32[]{:S(2)}) %collective-permute-start.9) | collective-permute-done | bytes 524320 | tf_op jit(solution)/shard_map/ppermute | solution.py:294
  61.3 4.2 %shard_map.54 = (bf16[8,8,4,48,512]{4,3,2,1,0:T(8,128)(2,1)}, bf16[8,448,512]{2,1,0:T(8,128)(2,1)}) custom-call(bf16[2560,512]{1,0:T(8,128)(2,1)S(1)} %get-tuple-element.40.rows_ref.own_ref, bf16[2560,512]{1,0:T(8,128)(2,1)S(1)} %collective-permute-done.8.other_ref, ...), custom_call_target="tpu_custom_call", output_to_operand_aliasing={{0}: (4, {})} | custom-call | flops 1024 | bytes 1024 | tf_op jit(solution)/shard_map/pallas_call | solution.py:272
  (10 shorter events, 0.2 us)
Async XLA Ops:
  3.2 24.0 %all-to-all-start = ((bf16[32,16,640]{2,1,0:T(8,128)(2,1)}), bf16[32,16,640]{2,1,0:T(8,128)(2,1)S(1)}, u32[]{:S(2)}, u32[]{:S(2)}) async-start(bf16[32,16,640]{2,1,0:T(8,128)(2,1)} %get-tuple-element.23), calls=%async_computation | async-start | bytes 1310720 | tf_op jit(solution)/shard_map/all_to_all | solution.py:298
  12.8 8.5 %collective-permute-start = (bf16[64,1792]{1,0:T(8,128)(2,1)}, bf16[64,1792]{1,0:T(8,128)(2,1)S(1)}, u32[]{:S(2)}, u32[]{:S(2)}) collective-permute-start(bf16[64,1792]{1,0:T(8,128)(2,1)} %get-tuple-element.25), channel_id=1, source_target_pairs={{0,4},{1,5},{2,6},{3,7},{4,8},{5,9},{6,10},{7,11},{8,12},{9,13},{1... | collective-permute-start | bytes 688136 | tf_op jit(solution)/shard_map/ppermute | solution.py:294
  14.1 13.1 %collective-permute-start.1 = (bf16[64,1792]{1,0:T(8,128)(2,1)}, bf16[64,1792]{1,0:T(8,128)(2,1)S(1)}, u32[]{:S(2)}, u32[]{:S(2)}) collective-permute-start(bf16[64,1792]{1,0:T(8,128)(2,1)} %get-tuple-element.26), channel_id=1, source_target_pairs={{0,8},{1,9},{2,10},{3,11},{4,12},{5,13},{6,14},{7,15},{8,0},{9,1},... | collective-permute-start | bytes 688136 | tf_op jit(solution)/shard_map/ppermute | solution.py:294
  16.5 10.6 %collective-permute-start.2 = (bf16[64,1792]{1,0:T(8,128)(2,1)}, bf16[64,1792]{1,0:T(8,128)(2,1)S(1)}, u32[]{:S(2)}, u32[]{:S(2)}) collective-permute-start(bf16[64,1792]{1,0:T(8,128)(2,1)} %get-tuple-element.27), channel_id=1, source_target_pairs={{0,12},{1,13},{2,14},{3,15},{4,0},{5,1},{6,2},{7,3},{8,4},{9,5},{1... | collective-permute-start | bytes 688136 | tf_op jit(solution)/shard_map/ppermute | solution.py:294
  27.6 10.8 %collective-permute-start.5 = (bf16[368,512]{1,0:T(8,128)(2,1)S(1)}, bf16[368,512]{1,0:T(8,128)(2,1)S(1)}, u32[]{:S(2)}, u32[]{:S(2)}) collective-permute-start(bf16[368,512]{1,0:T(8,128)(2,1)S(1)} %get-tuple-element.30), channel_id=1, source_target_pairs={{0,8},{1,9},{2,10},{3,11},{4,12},{5,13},{6,14},{7,15},{8,0},{9,1},... | collective-permute-start | bytes 1130504 | tf_op jit(solution)/shard_map/ppermute | solution.py:294
  29.9 23.4 %collective-permute-start.4 = (bf16[640,512]{1,0:T(8,128)(2,1)S(1)}, bf16[640,512]{1,0:T(8,128)(2,1)S(1)}, u32[]{:S(2)}, u32[]{:S(2)}) collective-permute-start(bf16[640,512]{1,0:T(8,128)(2,1)S(1)} %get-tuple-element.29.own), channel_id=1, source_target_pairs={{0,12},{1,13},{2,14},{3,15},{4,0},{5,1},{6,2},{7,3},{8,4},{9,5},{1... | collective-permute-start | bytes 1966088 | tf_op jit(solution)/shard_map/ppermute | solution.py:294
  31.2 22.8 %collective-permute-start.3 = (bf16[640,512]{1,0:T(8,128)(2,1)S(1)}, bf16[640,512]{1,0:T(8,128)(2,1)S(1)}, u32[]{:S(2)}, u32[]{:S(2)}) collective-permute-start(bf16[640,512]{1,0:T(8,128)(2,1)S(1)} %get-tuple-element.29.own), channel_id=1, source_target_pairs={{0,4},{1,5},{2,6},{3,7},{4,8},{5,9},{6,10},{7,11},{8,12},{9,13},{1... | collective-permute-start | bytes 1966088 | tf_op jit(solution)/shard_map/ppermute | solution.py:294
  32.6 11.4 %collective-permute-start.7 = (bf16[4,64,896]{2,1,0:T(8,128)(2,1)S(1)}, bf16[4,64,896]{2,1,0:T(8,128)(2,1)S(1)}, u32[]{:S(2)}, u32[]{:S(2)}) collective-permute-start(bf16[4,64,896]{2,1,0:T(8,128)(2,1)S(1)} %pad_maximum_fusion.1), channel_id=1, source_target_pairs={{0,2},{1,3},{2,0},{3,1},{4,6},{5,7},{6,4},{7,5},{8,10},{9,11},{10,... | collective-permute-start | bytes 1376264 | tf_op jit(solution)/shard_map/ppermute | solution.py:294
  38.5 15.5 %collective-permute-start.6 = (bf16[368,512]{1,0:T(8,128)(2,1)S(1)}, bf16[368,512]{1,0:T(8,128)(2,1)S(1)}, u32[]{:S(2)}, u32[]{:S(2)}) collective-permute-start(bf16[368,512]{1,0:T(8,128)(2,1)S(1)} %collective-permute-done.5.same_ref), channel_id=1, source_target_pairs={{0,2},{1,3},{2,0},{3,1},{4,6},{5,7},{6,4},{7,5},{8,10},{9,11},{10,... | collective-permute-start | bytes 1130504 | tf_op jit(solution)/shard_map/ppermute | solution.py:294
  54.8 6.6 %collective-permute-start.8 = (bf16[2560,512]{1,0:T(8,128)(2,1)S(1)}, bf16[2560,512]{1,0:T(8,128)(2,1)S(1)}, u32[]{:S(2)}, u32[]{:S(2)}) collective-permute-start(bf16[2560,512]{1,0:T(8,128)(2,1)S(1)} %get-tuple-element.40.rows_ref.own_ref), channel_id=1, source_target_pairs={{0,1},{1,0},{2,3},{3,2},{4,5},{5,4},{6,7},{7,6},{8,9},{9,8},{10,11... | collective-permute-start | bytes 7864328 | tf_op jit(solution)/shard_map/ppermute | solution.py:294
  56.1 5.3 %collective-permute-start.9 = (bf16[2,4,64,512]{3,2,1,0:T(8,128)(2,1)S(1)}, bf16[2,4,64,512]{3,2,1,0:T(8,128)(2,1)S(1)}, u32[]{:S(2)}, u32[]{:S(2)}) collective-permute-start(bf16[2,4,64,512]{3,2,1,0:T(8,128)(2,1)S(1)} %get-tuple-element.41), channel_id=1, source_target_pairs={{0,1},{1,0},{2,3},{3,2},{4,5},{5,4},{6,7},{7,6},{8,9},{9,8},{10,11... | collective-permute-start | bytes 1572872 | tf_op jit(solution)/shard_map/ppermute | solution.py:294
